TPU v7x, 128 devices: a whole 4x4x4 slice. The times are simulated.
128 devices in a mesh: inner: 4 (over x_lo, core), outer: 32 (over y, z, x_hi).
Axes of the slice: x: 4 (x_hi: 2, x_lo: 2; x = x_hi * 2 + x_lo), y: 4, z: 4, core: 2. Of those that a mesh axis runs over, the one named last changes fastest.
Arguments:
- query_rows: bfloat16 [32768, 6144], P(('inner', 'outer')), may hold values from -16 to 16
- key_rows: bfloat16 [32768, 1024], P(('inner', 'outer')), may hold values from -16 to 16
- value_rows: bfloat16 [32768, 1024], P(('inner', 'outer')), may hold values from -6 to 6
- out_grad: bfloat16 [32768, 6144], P(('inner', 'outer')), may hold values from -6 to 6
- doc_lengths: int32 [64], replicated, may hold values from 1 to 1025, 32768 in all
Outputs:
- attn_out: bfloat16 [32768, 6144], P(('inner', 'outer'))
- grad_query: bfloat16 [32768, 6144], P(('inner', 'outer'))
- grad_key: bfloat16 [32768, 1024], P(('inner', 'outer'))
- grad_value: bfloat16 [32768, 1024], P(('inner', 'outer'))
Inputs may be any that keep to these rules, and one draw needn't show every extreme that they name: `doc_lengths`: the lengths, in order, of the 64 documents packed into the sequence; they sum to 32768.
All inputs are finite; a program needn't handle non-finite values.
Results may differ from a plain program's by a relative error of at most 0.014.
Values may be sent and summed in bfloat16 or wider, within the bound.
No kernel may reach another device: no remote copies, remote signals or barrier semaphores. Data moves between devices by JAX's collectives and lax.ppermute only.
A program may use at most 192 MiB of HBM per device.

v0:
```python
import jax
import jax.numpy as jnp
from jax import lax
from jax.sharding import PartitionSpec as P

KVH = 8
GROUP = 6
DH = 128
REACH = 4


def shifted(value, axis, steps):
    count = lax.axis_size(axis)
    initial, last = (max(0, -steps), min(count, count - steps))
    return lax.ppermute(value, axis, [(source, source + steps) for source in range(initial, last)])


def document_of(doc_lengths, positions):
    boundaries = jnp.cumsum(doc_lengths, dtype=jnp.int32)
    hits = (boundaries[None, :] <= positions[:, None]).astype(jnp.int32)
    return jnp.sum(hits, axis=1, dtype=jnp.int32)


def guarded(kernel, inputs):
    return kernel(*inputs)


def dweight_piece(grad_group, value_piece):
    return jnp.einsum("tgd,wd->gtw", grad_group, value_piece, preferred_element_type=jnp.float32)


def tail_piece(weight_piece, dscore_piece, key_piece, value_piece, query_group, grad_group):
    out_part = jnp.einsum(
        "gtw,wd->tgd", weight_piece, value_piece, preferred_element_type=jnp.float32
    )
    query_part = jnp.einsum(
        "gtw,wd->tgd", dscore_piece, key_piece, preferred_element_type=jnp.float32
    )
    key_part = jnp.einsum(
        "gtw,tgd->wd", dscore_piece, query_group, preferred_element_type=jnp.float32
    )
    value_part = jnp.einsum(
        "gtw,tgd->wd", weight_piece, grad_group, preferred_element_type=jnp.float32
    )
    return (out_part, query_part, key_part, value_part)


def on_device(query_rows, key_rows, value_rows, out_grad, doc_lengths):
    tok_rows = query_rows.shape[0]
    slot_count = REACH + 1
    window_rows = slot_count * tok_rows
    group_cols = GROUP * DH
    score_scale = DH ** (-0.5)
    my_index = lax.axis_index(("inner", "outer"))
    kv_pair = jnp.stack([key_rows, value_rows])
    received = [kv_pair]
    moving = kv_pair
    for distance in range(1, REACH + 1):
        moving = shifted(moving, ("inner", "outer"), 1)
        received.append(moving)
    window = jnp.concatenate(received[::-1], axis=1)
    query_pos = my_index * tok_rows + jnp.arange(tok_rows, dtype=jnp.int32)
    key_pos = (my_index - REACH) * tok_rows + jnp.arange(window_rows, dtype=jnp.int32)
    same_doc = (
        document_of(doc_lengths, query_pos)[:, None] == document_of(doc_lengths, key_pos)[None, :]
    )
    allowed = same_doc & (key_pos[None, :] <= query_pos[:, None]) & (key_pos[None, :] >= 0)

    def score_piece(query_group, key_piece):
        return (
            jnp.einsum("tgd,wd->gtw", query_group, key_piece, preferred_element_type=jnp.float32)
            * score_scale
        )

    def one_group(group_index, carried):
        out_all, dquery_all, dkey_all, dvalue_all = carried
        query_group = lax.dynamic_slice_in_dim(
            query_rows, group_index * group_cols, group_cols, 1
        ).reshape(tok_rows, GROUP, DH)
        grad_group = lax.dynamic_slice_in_dim(
            out_grad, group_index * group_cols, group_cols, 1
        ).reshape(tok_rows, GROUP, DH)
        key_group = lax.dynamic_slice_in_dim(window[0], group_index * DH, DH, 1)
        value_group = lax.dynamic_slice_in_dim(window[1], group_index * DH, DH, 1)
        key_pieces = [
            key_group[slot_index * tok_rows : (slot_index + 1) * tok_rows]
            for slot_index in range(slot_count)
        ]
        value_pieces = [
            value_group[slot_index * tok_rows : (slot_index + 1) * tok_rows]
            for slot_index in range(slot_count)
        ]
        score_list = [
            guarded(score_piece, (query_group, key_pieces[slot_index]))
            for slot_index in range(slot_count)
        ]
        scores = jnp.where(allowed[None], jnp.concatenate(score_list, axis=2), -jnp.inf)
        row_peak = jnp.max(scores, axis=2, keepdims=True)
        exp_scores = jnp.exp(scores - row_peak)
        probs = exp_scores / jnp.sum(exp_scores, axis=2, keepdims=True)
        weights = probs.astype(jnp.bfloat16)
        dweight_list = [
            guarded(dweight_piece, (grad_group, value_pieces[slot_index]))
            for slot_index in range(slot_count)
        ]
        dweights = jnp.concatenate(dweight_list, axis=2)
        row_delta = jnp.sum(probs * dweights, axis=2, keepdims=True)
        dscores = (probs * (dweights - row_delta) * score_scale).astype(jnp.bfloat16)
        out_sum = jnp.zeros((tok_rows, GROUP, DH), jnp.float32)
        dquery_sum = jnp.zeros((tok_rows, GROUP, DH), jnp.float32)
        key_parts = []
        value_parts = []
        for slot_index in range(slot_count):
            lower = slot_index * tok_rows
            upper = lower + tok_rows
            inputs = (
                weights[:, :, lower:upper],
                dscores[:, :, lower:upper],
                key_pieces[slot_index],
                value_pieces[slot_index],
                query_group,
                grad_group,
            )
            out_part, query_part, key_part, value_part = guarded(tail_piece, inputs)
            out_sum = out_sum + out_part
            dquery_sum = dquery_sum + query_part
            key_parts.append(key_part)
            value_parts.append(value_part)
        out_all = lax.dynamic_update_slice_in_dim(
            out_all,
            out_sum.reshape(tok_rows, group_cols).astype(jnp.bfloat16),
            group_index * group_cols,
            1,
        )
        dquery_all = lax.dynamic_update_slice_in_dim(
            dquery_all,
            dquery_sum.reshape(tok_rows, group_cols).astype(jnp.bfloat16),
            group_index * group_cols,
            1,
        )
        dkey_all = lax.dynamic_update_slice_in_dim(
            dkey_all, jnp.concatenate(key_parts, axis=0).astype(jnp.bfloat16), group_index * DH, 1
        )
        dvalue_all = lax.dynamic_update_slice_in_dim(
            dvalue_all,
            jnp.concatenate(value_parts, axis=0).astype(jnp.bfloat16),
            group_index * DH,
            1,
        )
        return (out_all, dquery_all, dkey_all, dvalue_all)

    start_state = (
        jnp.zeros((tok_rows, KVH * group_cols), jnp.bfloat16),
        jnp.zeros((tok_rows, KVH * group_cols), jnp.bfloat16),
        jnp.zeros((window_rows, KVH * DH), jnp.bfloat16),
        jnp.zeros((window_rows, KVH * DH), jnp.bfloat16),
    )
    attn_out, grad_query, dkey_all, dvalue_all = lax.fori_loop(0, KVH, one_group, start_state)
    grad_window = jnp.stack([dkey_all, dvalue_all])

    def grad_slice(distance):
        lower = (REACH - distance) * tok_rows
        return grad_window[:, lower : lower + tok_rows]

    summed = lax.optimization_barrier(grad_slice(0)).astype(jnp.float32)
    moving = jnp.stack([grad_slice(distance) for distance in range(1, REACH + 1)])
    for distance in range(1, REACH + 1):
        moving = shifted(moving, ("inner", "outer"), -1)
        summed = summed + moving[0].astype(jnp.float32)
        moving = moving[1:]
    grad_key = summed[0].astype(jnp.bfloat16)
    grad_value = summed[1].astype(jnp.bfloat16)
    return (attn_out, grad_query, grad_key, grad_value)


def solution(mesh):
    in_specs = (
        P(("inner", "outer"), None),
        P(("inner", "outer"), None),
        P(("inner", "outer"), None),
        P(("inner", "outer"), None),
        P(),
    )
    out_specs = (
        P(("inner", "outer"), None),
        P(("inner", "outer"), None),
        P(("inner", "outer"), None),
        P(("inner", "outer"), None),
    )
    return jax.shard_map(
        on_device, mesh=mesh, in_specs=in_specs, out_specs=out_specs, check_vma=False
    )
```

profile of v0, /device:TPU:1, one launch (start us, length us, event | category | flops | bytes accessed | tf_op | source)
XLA Modules:
  0.0 1039.4 jit_solution(4488710997541645761)
XLA Ops:
  1.9 5.5 collective-permute-start
  7.4 21.8 %collective-permute-done = bf16[2,256,1024]{2,1,0:T(8,128)(2,1)S(1)} collective-permute-done((bf16[2,256,1024]{2,1,0:T(8,128)(2,1)S(1)}, bf16[2,256,1024]{2,1,0:T(8,128)(2,1)S(1)}, u32[]{:S(2)}, u32[]{:S(2)}) %collective-permute-start) | collective-permute-done | bytes 1048608 | tf_op jit(solution)/shard_map/ppermute | solution.py:15
  29.2 5.6 collective-permute-start.1
  34.8 20.9 %collective-permute-done.1 = bf16[2,256,1024]{2,1,0:T(8,128)(2,1)S(1)} collective-permute-done((bf16[2,256,1024]{2,1,0:T(8,128)(2,1)S(1)}, bf16[2,256,1024]{2,1,0:T(8,128)(2,1)S(1)}, u32[]{:S(2)}, u32[]{:S(2)}) %collective-permute-start.1) | collective-permute-done | bytes 1048608 | tf_op jit(solution)/shard_map/ppermute | solution.py:15
  55.7 5.6 collective-permute-start.2
  61.3 20.7 %collective-permute-done.2 = bf16[2,256,1024]{2,1,0:T(8,128)(2,1)S(1)} collective-permute-done((bf16[2,256,1024]{2,1,0:T(8,128)(2,1)S(1)}, bf16[2,256,1024]{2,1,0:T(8,128)(2,1)S(1)}, u32[]{:S(2)}, u32[]{:S(2)}) %collective-permute-start.2) | collective-permute-done | bytes 1048608 | tf_op jit(solution)/shard_map/ppermute | solution.py:15
  82.1 4.8 collective-permute-start.3
  88.1 21.3 %collective-permute-done.3 = bf16[2,256,1024]{2,1,0:T(8,128)(2,1)} collective-permute-done((bf16[2,256,1024]{2,1,0:T(8,128)(2,1)S(1)}, bf16[2,256,1024]{2,1,0:T(8,128)(2,1)}, u32[]{:S(2)}, u32[]{:S(2)}) %collective-permute-start.3) | collective-permute-done | bytes 1048608 | tf_op jit(solution)/shard_map/ppermute | solution.py:15
  123.7 670.9 %while.20 = (s32[]{:T(128)}, bf16[256,6144]{1,0:T(8,128)(2,1)}, bf16[256,6144]{1,0:T(8,128)(2,1)}, bf16[1280,1024]{1,0:T(8,128)(2,1)}, bf16[1280,1024]{1,0:T(8,1...) while((s32[]{:T(128)}, bf16[256,6144]{1,0:T(8,128)(2,1)}, ...), condition=%wide.region_7.8_spmd.clone, body=%wide.region_3.7_spmd.clone.sunk | while | flops 3051032576 | bytes 157318960 | solution.py:158
  135.6 11.6 %fusion.206 = (f32[6,256]{1,0:T(8,128)S(1)}, f32[6,256,1280]{1,2,0:T(8,128)}) fusion(f32[6,256,1280]{1,2,0:T(8,128)} %bitcast_dynamic-update-slice_fusion.29, pred[256,1280]{0,1:T(8,128)(4,1)S(1)} %and_and_fusion.2), kind=kOutput, calls=%fused_computation.162.clone.1 | output fusion | flops 7865599 | bytes 16062464 | tf_op jit(solution)/shard_map/while/body/eval_jaxpr/sub | solution.py:99
  150.1 7.9 copy.187
  168.0 14.2 %multiply_convert_fusion.2 = bf16[6,256,1280]{1,2,0:T(8,128)(2,1)} fusion(f32[6,256,1280]{1,2,0:T(8,128)} %bitcast_dynamic-update-slice_fusion.24, f32[6,256,1280]{1,2,0:T(8,128)} %get-tuple-element.360, f32[6,256]{1,0:T(8,128)S(1)} %get-tuple-element.361), kind=kOutput, calls=%fused_computation.3.clone.1 | output fusion | flops 13765375 | bytes 19666944 | tf_op jit(solution)/shard_map/while/body/eval_jaxpr/sub | solution.py:108
  189.8 3.9 fusion.209
  219.4 11.6 %fusion.206 = (f32[6,256]{1,0:T(8,128)S(1)}, f32[6,256,1280]{1,2,0:T(8,128)}) fusion(f32[6,256,1280]{1,2,0:T(8,128)} %bitcast_dynamic-update-slice_fusion.29, pred[256,1280]{0,1:T(8,128)(4,1)S(1)} %and_and_fusion.2), kind=kOutput, calls=%fused_computation.162.clone.1 | output fusion | flops 7865599 | bytes 16062464 | tf_op jit(solution)/shard_map/while/body/eval_jaxpr/sub | solution.py:99
  233.9 7.9 copy.187
  251.8 14.2 %multiply_convert_fusion.2 = bf16[6,256,1280]{1,2,0:T(8,128)(2,1)} fusion(f32[6,256,1280]{1,2,0:T(8,128)} %bitcast_dynamic-update-slice_fusion.24, f32[6,256,1280]{1,2,0:T(8,128)} %get-tuple-element.360, f32[6,256]{1,0:T(8,128)S(1)} %get-tuple-element.361), kind=kOutput, calls=%fused_computation.3.clone.1 | output fusion | flops 13765375 | bytes 19666944 | tf_op jit(solution)/shard_map/while/body/eval_jaxpr/sub | solution.py:108
  273.6 3.9 fusion.209
  303.3 11.6 %fusion.206 = (f32[6,256]{1,0:T(8,128)S(1)}, f32[6,256,1280]{1,2,0:T(8,128)}) fusion(f32[6,256,1280]{1,2,0:T(8,128)} %bitcast_dynamic-update-slice_fusion.29, pred[256,1280]{0,1:T(8,128)(4,1)S(1)} %and_and_fusion.2), kind=kOutput, calls=%fused_computation.162.clone.1 | output fusion | flops 7865599 | bytes 16062464 | tf_op jit(solution)/shard_map/while/body/eval_jaxpr/sub | solution.py:99
  317.8 7.9 copy.187
  335.7 14.2 %multiply_convert_fusion.2 = bf16[6,256,1280]{1,2,0:T(8,128)(2,1)} fusion(f32[6,256,1280]{1,2,0:T(8,128)} %bitcast_dynamic-update-slice_fusion.24, f32[6,256,1280]{1,2,0:T(8,128)} %get-tuple-element.360, f32[6,256]{1,0:T(8,128)S(1)} %get-tuple-element.361), kind=kOutput, calls=%fused_computation.3.clone.1 | output fusion | flops 13765375 | bytes 19666944 | tf_op jit(solution)/shard_map/while/body/eval_jaxpr/sub | solution.py:108
  357.5 3.9 fusion.209
  387.1 11.6 %fusion.206 = (f32[6,256]{1,0:T(8,128)S(1)}, f32[6,256,1280]{1,2,0:T(8,128)}) fusion(f32[6,256,1280]{1,2,0:T(8,128)} %bitcast_dynamic-update-slice_fusion.29, pred[256,1280]{0,1:T(8,128)(4,1)S(1)} %and_and_fusion.2), kind=kOutput, calls=%fused_computation.162.clone.1 | output fusion | flops 7865599 | bytes 16062464 | tf_op jit(solution)/shard_map/while/body/eval_jaxpr/sub | solution.py:99
  401.6 7.9 copy.187
  419.5 14.2 %multiply_convert_fusion.2 = bf16[6,256,1280]{1,2,0:T(8,128)(2,1)} fusion(f32[6,256,1280]{1,2,0:T(8,128)} %bitcast_dynamic-update-slice_fusion.24, f32[6,256,1280]{1,2,0:T(8,128)} %get-tuple-element.360, f32[6,256]{1,0:T(8,128)S(1)} %get-tuple-element.361), kind=kOutput, calls=%fused_computation.3.clone.1 | output fusion | flops 13765375 | bytes 19666944 | tf_op jit(solution)/shard_map/while/body/eval_jaxpr/sub | solution.py:108
  441.3 3.9 fusion.209
  471.0 11.6 %fusion.206 = (f32[6,256]{1,0:T(8,128)S(1)}, f32[6,256,1280]{1,2,0:T(8,128)}) fusion(f32[6,256,1280]{1,2,0:T(8,128)} %bitcast_dynamic-update-slice_fusion.29, pred[256,1280]{0,1:T(8,128)(4,1)S(1)} %and_and_fusion.2), kind=kOutput, calls=%fused_computation.162.clone.1 | output fusion | flops 7865599 | bytes 16062464 | tf_op jit(solution)/shard_map/while/body/eval_jaxpr/sub | solution.py:99
  485.5 7.9 copy.187
  503.4 14.2 %multiply_convert_fusion.2 = bf16[6,256,1280]{1,2,0:T(8,128)(2,1)} fusion(f32[6,256,1280]{1,2,0:T(8,128)} %bitcast_dynamic-update-slice_fusion.24, f32[6,256,1280]{1,2,0:T(8,128)} %get-tuple-element.360, f32[6,256]{1,0:T(8,128)S(1)} %get-tuple-element.361), kind=kOutput, calls=%fused_computation.3.clone.1 | output fusion | flops 13765375 | bytes 19666944 | tf_op jit(solution)/shard_map/while/body/eval_jaxpr/sub | solution.py:108
  525.2 3.9 fusion.209
  554.8 11.6 %fusion.206 = (f32[6,256]{1,0:T(8,128)S(1)}, f32[6,256,1280]{1,2,0:T(8,128)}) fusion(f32[6,256,1280]{1,2,0:T(8,128)} %bitcast_dynamic-update-slice_fusion.29, pred[256,1280]{0,1:T(8,128)(4,1)S(1)} %and_and_fusion.2), kind=kOutput, calls=%fused_computation.162.clone.1 | output fusion | flops 7865599 | bytes 16062464 | tf_op jit(solution)/shard_map/while/body/eval_jaxpr/sub | solution.py:99
  569.3 7.9 copy.187
  587.2 14.2 %multiply_convert_fusion.2 = bf16[6,256,1280]{1,2,0:T(8,128)(2,1)} fusion(f32[6,256,1280]{1,2,0:T(8,128)} %bitcast_dynamic-update-slice_fusion.24, f32[6,256,1280]{1,2,0:T(8,128)} %get-tuple-element.360, f32[6,256]{1,0:T(8,128)S(1)} %get-tuple-element.361), kind=kOutput, calls=%fused_computation.3.clone.1 | output fusion | flops 13765375 | bytes 19666944 | tf_op jit(solution)/shard_map/while/body/eval_jaxpr/sub | solution.py:108
  609.0 3.9 fusion.209
  638.7 11.6 %fusion.206 = (f32[6,256]{1,0:T(8,128)S(1)}, f32[6,256,1280]{1,2,0:T(8,128)}) fusion(f32[6,256,1280]{1,2,0:T(8,128)} %bitcast_dynamic-update-slice_fusion.29, pred[256,1280]{0,1:T(8,128)(4,1)S(1)} %and_and_fusion.2), kind=kOutput, calls=%fused_computation.162.clone.1 | output fusion | flops 7865599 | bytes 16062464 | tf_op jit(solution)/shard_map/while/body/eval_jaxpr/sub | solution.py:99
  653.2 7.9 copy.187
  671.1 14.2 %multiply_convert_fusion.2 = bf16[6,256,1280]{1,2,0:T(8,128)(2,1)} fusion(f32[6,256,1280]{1,2,0:T(8,128)} %bitcast_dynamic-update-slice_fusion.24, f32[6,256,1280]{1,2,0:T(8,128)} %get-tuple-element.360, f32[6,256]{1,0:T(8,128)S(1)} %get-tuple-element.361), kind=kOutput, calls=%fused_computation.3.clone.1 | output fusion | flops 13765375 | bytes 19666944 | tf_op jit(solution)/shard_map/while/body/eval_jaxpr/sub | solution.py:108
  692.9 3.9 fusion.209
  722.6 11.6 %fusion.206 = (f32[6,256]{1,0:T(8,128)S(1)}, f32[6,256,1280]{1,2,0:T(8,128)}) fusion(f32[6,256,1280]{1,2,0:T(8,128)} %bitcast_dynamic-update-slice_fusion.29, pred[256,1280]{0,1:T(8,128)(4,1)S(1)} %and_and_fusion.2), kind=kOutput, calls=%fused_computation.162.clone.1 | output fusion | flops 7865599 | bytes 16062464 | tf_op jit(solution)/shard_map/while/body/eval_jaxpr/sub | solution.py:99
  737.1 7.9 copy.187
  755.0 14.2 %multiply_convert_fusion.2 = bf16[6,256,1280]{1,2,0:T(8,128)(2,1)} fusion(f32[6,256,1280]{1,2,0:T(8,128)} %bitcast_dynamic-update-slice_fusion.24, f32[6,256,1280]{1,2,0:T(8,128)} %get-tuple-element.360, f32[6,256]{1,0:T(8,128)S(1)} %get-tuple-element.361), kind=kOutput, calls=%fused_computation.3.clone.1 | output fusion | flops 13765375 | bytes 19666944 | tf_op jit(solution)/shard_map/while/body/eval_jaxpr/sub | solution.py:108
  798.0 15.0 %collective-permute-start.4 = (bf16[4,2,256,1024]{3,2,1,0:T(8,128)(2,1)S(1)}, bf16[4,2,256,1024]{3,2,1,0:T(8,128)(2,1)S(1)}, u32[]{:S(2)}, u32[]{:S(2)}) collective-permute-start(bf16[4,2,256,1024]{3,2,1,0:T(8,128)(2,1)S(1)} %pad_maximum_fusion), channel_id=1, source_target_pairs={{1,0},{2,1},{3,2},{4,3},{5,4},{6,5},{7,6},{8,7},{9,8},{10,9},{11,1... | collective-permute-start | bytes 12582920 | tf_op jit(solution)/shard_map/ppermute | solution.py:15
  812.9 78.6 %collective-permute-done.4 = bf16[4,2,256,1024]{3,2,1,0:T(8,128)(2,1)S(1)} collective-permute-done((bf16[4,2,256,1024]{3,2,1,0:T(8,128)(2,1)S(1)}, bf16[4,2,256,1024]{3,2,1,0:T(8,128)(2,1)S(1)}, u32[]{:S(2)}, u32[]{:S(2)}) %collective-permute-start.4) | collective-permute-done | bytes 4194336 | tf_op jit(solution)/shard_map/ppermute | solution.py:15
  892.1 11.6 %collective-permute-start.5 = (bf16[3,2,256,1024]{3,2,1,0:T(8,128)(2,1)S(1)}, bf16[3,2,256,1024]{3,2,1,0:T(8,128)(2,1)S(1)}, u32[]{:S(2)}, u32[]{:S(2)}) collective-permute-start(bf16[3,2,256,1024]{3,2,1,0:T(8,128)(2,1)S(1)} %slice.290), channel_id=1, source_target_pairs={{1,0},{2,1},{3,2},{4,3},{5,4},{6,5},{7,6},{8,7},{9,8},{10,9},{11,1... | collective-permute-start | bytes 9437192 | tf_op jit(solution)/shard_map/ppermute | solution.py:15
  903.7 58.6 %collective-permute-done.5 = bf16[3,2,256,1024]{3,2,1,0:T(8,128)(2,1)S(1)} collective-permute-done((bf16[3,2,256,1024]{3,2,1,0:T(8,128)(2,1)S(1)}, bf16[3,2,256,1024]{3,2,1,0:T(8,128)(2,1)S(1)}, u32[]{:S(2)}, u32[]{:S(2)}) %collective-permute-start.5) | collective-permute-done | bytes 3145760 | tf_op jit(solution)/shard_map/ppermute | solution.py:15
  962.5 12.8 %collective-permute-start.6 = (bf16[2,2,256,1024]{3,2,1,0:T(8,128)(2,1)S(1)}, bf16[2,2,256,1024]{3,2,1,0:T(8,128)(2,1)S(1)}, u32[]{:S(2)}, u32[]{:S(2)}) collective-permute-start(bf16[2,2,256,1024]{3,2,1,0:T(8,128)(2,1)S(1)} %slice.292), channel_id=1, source_target_pairs={{1,0},{2,1},{3,2},{4,3},{5,4},{6,5},{7,6},{8,7},{9,8},{10,9},{11,1... | collective-permute-start | bytes 6291464 | tf_op jit(solution)/shard_map/ppermute | solution.py:15
  975.3 34.0 %collective-permute-done.6 = bf16[2,2,256,1024]{3,2,1,0:T(8,128)(2,1)S(1)} collective-permute-done((bf16[2,2,256,1024]{3,2,1,0:T(8,128)(2,1)S(1)}, bf16[2,2,256,1024]{3,2,1,0:T(8,128)(2,1)S(1)}, u32[]{:S(2)}, u32[]{:S(2)}) %collective-permute-start.6) | collective-permute-done | bytes 2097184 | tf_op jit(solution)/shard_map/ppermute | solution.py:15
  1009.4 16.0 %collective-permute-start.7 = (bf16[1,2,256,1024]{3,2,1,0:T(8,128)(2,1)S(1)}, bf16[1,2,256,1024]{3,2,1,0:T(8,128)(2,1)S(1)}, u32[]{:S(2)}, u32[]{:S(2)}) collective-permute-start(bf16[1,2,256,1024]{3,2,1,0:T(8,128)(2,1)S(1)} %slice.294), channel_id=1, source_target_pairs={{1,0},{2,1},{3,2},{4,3},{5,4},{6,5},{7,6},{8,7},{9,8},{10,9},{11,1... | collective-permute-start | bytes 3145736 | tf_op jit(solution)/shard_map/ppermute | solution.py:15
  1025.5 11.8 %collective-permute-done.7 = bf16[1,2,256,1024]{3,2,1,0:T(8,128)(2,1)S(1)} collective-permute-done((bf16[1,2,256,1024]{3,2,1,0:T(8,128)(2,1)S(1)}, bf16[1,2,256,1024]{3,2,1,0:T(8,128)(2,1)S(1)}, u32[]{:S(2)}, u32[]{:S(2)}) %collective-permute-start.7) | collective-permute-done | bytes 1048608 | tf_op jit(solution)/shard_map/ppermute | solution.py:15
  (390 shorter events, 396.3 us)
Async XLA Ops:
  1.9 27.3 %collective-permute-start = (bf16[2,256,1024]{2,1,0:T(8,128)(2,1)S(1)}, bf16[2,256,1024]{2,1,0:T(8,128)(2,1)S(1)}, u32[]{:S(2)}, u32[]{:S(2)}) collective-permute-start(bf16[2,256,1024]{2,1,0:T(8,128)(2,1)S(1)} %pad_maximum_fusion.2), channel_id=1, source_target_pairs={{0,1},{1,2},{2,3},{3,4},{4,5},{5,6},{6,7},{7,8},{8,9},{9,10},{10,1... | collective-permute-start | bytes 3145736 | tf_op jit(solution)/shard_map/ppermute | solution.py:15
  29.2 26.5 %collective-permute-start.1 = (bf16[2,256,1024]{2,1,0:T(8,128)(2,1)S(1)}, bf16[2,256,1024]{2,1,0:T(8,128)(2,1)S(1)}, u32[]{:S(2)}, u32[]{:S(2)}) collective-permute-start(bf16[2,256,1024]{2,1,0:T(8,128)(2,1)S(1)} %collective-permute-done), channel_id=1, source_target_pairs={{0,1},{1,2},{2,3},{3,4},{4,5},{5,6},{6,7},{7,8},{8,9},{9,10},{10,1... | collective-permute-start | bytes 3145736 | tf_op jit(solution)/shard_map/ppermute | solution.py:15
  55.7 26.4 %collective-permute-start.2 = (bf16[2,256,1024]{2,1,0:T(8,128)(2,1)S(1)}, bf16[2,256,1024]{2,1,0:T(8,128)(2,1)S(1)}, u32[]{:S(2)}, u32[]{:S(2)}) collective-permute-start(bf16[2,256,1024]{2,1,0:T(8,128)(2,1)S(1)} %collective-permute-done.1), channel_id=1, source_target_pairs={{0,1},{1,2},{2,3},{3,4},{4,5},{5,6},{6,7},{7,8},{8,9},{9,10},{10,1... | collective-permute-start | bytes 3145736 | tf_op jit(solution)/shard_map/ppermute | solution.py:15
  82.1 27.3 %collective-permute-start.3 = (bf16[2,256,1024]{2,1,0:T(8,128)(2,1)S(1)}, bf16[2,256,1024]{2,1,0:T(8,128)(2,1)}, u32[]{:S(2)}, u32[]{:S(2)}) collective-permute-start(bf16[2,256,1024]{2,1,0:T(8,128)(2,1)S(1)} %collective-permute-done.2), channel_id=1, source_target_pairs={{0,1},{1,2},{2,3},{3,4},{4,5},{5,6},{6,7},{7,8},{8,9},{9,10},{10,1... | collective-permute-start | bytes 3145736 | tf_op jit(solution)/shard_map/ppermute | solution.py:15
  88.1 26.8 %copy-start.2 = (bf16[256,1024]{1,0:T(8,128)(2,1)S(1)}, bf16[256,1024]{1,0:T(8,128)(2,1)}, u32[]{:S(2)}) copy-start(bf16[256,1024]{1,0:T(8,128)(2,1)} %param.9) | copy-start | bytes 1572868
  88.1 26.7 %copy-start.3 = (bf16[256,1024]{1,0:T(8,128)(2,1)S(1)}, bf16[256,1024]{1,0:T(8,128)(2,1)}, u32[]{:S(2)}) copy-start(bf16[256,1024]{1,0:T(8,128)(2,1)} %param.8) | copy-start | bytes 1572868
  159.9 6.6 copy-start
  202.4 3.1 copy-start.1
  243.7 6.6 copy-start
  286.2 3.1 copy-start.1
  327.6 6.6 copy-start
  370.1 3.1 copy-start.1
  411.4 6.6 copy-start
  453.9 3.1 copy-start.1
  495.3 6.6 copy-start
  537.7 3.1 copy-start.1
  579.1 6.6 copy-start
  621.6 3.1 copy-start.1
  663.0 6.6 copy-start
  705.5 3.1 copy-start.1
  746.9 6.6 copy-start
  789.4 3.1 copy-start.1
  798.0 93.6 %collective-permute-start.4 = (bf16[4,2,256,1024]{3,2,1,0:T(8,128)(2,1)S(1)}, bf16[4,2,256,1024]{3,2,1,0:T(8,128)(2,1)S(1)}, u32[]{:S(2)}, u32[]{:S(2)}) collective-permute-start(bf16[4,2,256,1024]{3,2,1,0:T(8,128)(2,1)S(1)} %pad_maximum_fusion), channel_id=1, source_target_pairs={{1,0},{2,1},{3,2},{4,3},{5,4},{6,5},{7,6},{8,7},{9,8},{10,9},{11,1... | collective-permute-start | bytes 12582920 | tf_op jit(solution)/shard_map/ppermute | solution.py:15
  892.1 70.2 %collective-permute-start.5 = (bf16[3,2,256,1024]{3,2,1,0:T(8,128)(2,1)S(1)}, bf16[3,2,256,1024]{3,2,1,0:T(8,128)(2,1)S(1)}, u32[]{:S(2)}, u32[]{:S(2)}) collective-permute-start(bf16[3,2,256,1024]{3,2,1,0:T(8,128)(2,1)S(1)} %slice.290), channel_id=1, source_target_pairs={{1,0},{2,1},{3,2},{4,3},{5,4},{6,5},{7,6},{8,7},{9,8},{10,9},{11,1... | collective-permute-start | bytes 9437192 | tf_op jit(solution)/shard_map/ppermute | solution.py:15
  962.5 46.8 %collective-permute-start.6 = (bf16[2,2,256,1024]{3,2,1,0:T(8,128)(2,1)S(1)}, bf16[2,2,256,1024]{3,2,1,0:T(8,128)(2,1)S(1)}, u32[]{:S(2)}, u32[]{:S(2)}) collective-permute-start(bf16[2,2,256,1024]{3,2,1,0:T(8,128)(2,1)S(1)} %slice.292), channel_id=1, source_target_pairs={{1,0},{2,1},{3,2},{4,3},{5,4},{6,5},{7,6},{8,7},{9,8},{10,9},{11,1... | collective-permute-start | bytes 6291464 | tf_op jit(solution)/shard_map/ppermute | solution.py:15
  1009.4 27.8 %collective-permute-start.7 = (bf16[1,2,256,1024]{3,2,1,0:T(8,128)(2,1)S(1)}, bf16[1,2,256,1024]{3,2,1,0:T(8,128)(2,1)S(1)}, u32[]{:S(2)}, u32[]{:S(2)}) collective-permute-start(bf16[1,2,256,1024]{3,2,1,0:T(8,128)(2,1)S(1)} %slice.294), channel_id=1, source_target_pairs={{1,0},{2,1},{3,2},{4,3},{5,4},{6,5},{7,6},{8,7},{9,8},{10,9},{11,1... | collective-permute-start | bytes 3145736 | tf_op jit(solution)/shard_map/ppermute | solution.py:15
where the time goes:
time: 1060 us; the launch traced here: 1040 us
  matrix products  279 us (26%)
  waiting for transfers between devices  268 us (25%)
  other arithmetic  253 us (24%)
  local copies, waits for them, and re-layouts  161 us (15%)
  starting transfers between devices  76.9 us (7%)
    ppermute x8, waiting for transfers between devices, shifted(): lax.ppermute(value, axis, [(source, source + steps) for source in range(i...  268 us
    sub x8, other arithmetic, one_group(): dweights - row_delta  114 us
    sub x8, other arithmetic, one_group(): exp_scores = jnp.exp(scores - row_peak)  92.7 us
    ppermute x8, starting transfers between devices, shifted(): lax.ppermute(value, axis, [(source, source + steps) for source in range(i...  76.9 us
    dot_general x40, matrix products, dweight_piece(): jnp.einsum('tgd,wd->gtw', grad_group, value_piece, preferred_element_type...  64.7 us
    while x40, local copies, waits for them, and re-layouts  63 us
    dot_general x40, matrix products, score_piece(): jnp.einsum('tgd,wd->gtw', query_group, key_piece, preferred_element_type=...  61.3 us
    dot_general x40, matrix products, tail_piece(): jnp.einsum('gtw,tgd->wd', dscore_piece, query_group, preferred_element_ty...  60.8 us
  transfers between devices with their start and end apart: 8, of which 8 were waited for; matrix products, arithmetic and copies ran while one was open for 0% of the time, Pallas kernels for 0%

commit v1 on v0

v1 whole, which is shorter than its diff:
```python
import functools

import jax
import jax.numpy as jnp
from jax import lax
from jax.experimental import pallas as pl
from jax.experimental.pallas import tpu as pltpu
from jax.sharding import PartitionSpec as P

KVH = 8
GROUP = 6
DH = 128
REACH = 4
SLOTS = REACH + 1
TOK = 256
AXES = ("inner", "outer")
SCALE = DH ** (-0.5)
LOG2E = 1.4426950408889634
MASKED = -1e30
CHUNKS = 2
NN = (((1,), (0,)), ((), ()))
NT = (((1,), (1,)), ((), ()))


def mm(left, right, dims=NN):
    return lax.dot_general(left, right, dims, preferred_element_type=jnp.float32)


def attention_body(aliased, lo_ref, q_ref, g_ref, *refs):
    kv = refs[:SLOTS]
    refs = refs[SLOTS + aliased :]
    out_ref, dq_ref = refs[:2]
    dkv = refs[2 : 2 + SLOTS]
    bias_ref, t_ref, w_ref, ds_ref = refs[2 + SLOTS :]

    @pl.when(pl.program_id(0) == 0)
    def _():
        lo = lo_ref[...]
        qpos = lax.broadcasted_iota(jnp.int32, (TOK, TOK), 1)
        kpos = lax.broadcasted_iota(jnp.int32, (TOK, TOK), 0)
        for d in range(SLOTS):
            k = kpos - d * TOK
            ok = (k >= lo) & (k <= qpos)
            bias_ref[d] = jnp.where(ok, 0.0, MASKED)

    for h in range(GROUP):
        cols = slice(h * DH, (h + 1) * DH)
        qc = slice(h * TOK, (h + 1) * TOK)
        q = q_ref[:, cols]
        g = g_ref[:, cols]
        peak = None
        for d in range(SLOTS):
            t = mm(kv[d][0], q, NT) * (SCALE * LOG2E) + bias_ref[d]
            t_ref[d] = t
            part = jnp.max(t, axis=0, keepdims=True)
            peak = part if peak is None else jnp.maximum(peak, part)
        total = None
        for d in range(SLOTS):
            e = jnp.exp2(t_ref[d] - peak)
            t_ref[d] = e
            part = jnp.sum(e, axis=0, keepdims=True)
            total = part if total is None else total + part
        inverse = 1.0 / total
        out = None
        for d in range(SLOTS):
            p = t_ref[d] * inverse
            t_ref[d] = p
            w = p.astype(jnp.bfloat16)
            w_ref[d, :, qc] = w
            part = mm(kv[d][1].T, w)
            out = part if out is None else out + part
        out_ref[:, cols] = out.T.astype(jnp.bfloat16)
        delta = jnp.sum(out * g.astype(jnp.float32).T, axis=0, keepdims=True)
        dq = None
        for d in range(SLOTS):
            dp = mm(kv[d][1], g, NT)
            s = (t_ref[d] * (dp - delta)).astype(jnp.bfloat16)
            ds_ref[d, :, qc] = s
            part = mm(kv[d][0].T, s)
            dq = part if dq is None else dq + part
        dq_ref[:, cols] = (dq * SCALE).T.astype(jnp.bfloat16)
    qs = jnp.concatenate([q_ref[:, h * DH : (h + 1) * DH] for h in range(GROUP)], axis=0)
    gs = jnp.concatenate([g_ref[:, h * DH : (h + 1) * DH] for h in range(GROUP)], axis=0)
    for d in range(SLOTS):
        dkv[d][0] = (mm(ds_ref[d], qs) * SCALE).astype(jnp.bfloat16)
        dkv[d][1] = mm(w_ref[d], gs).astype(jnp.bfloat16)


def attend(lo, query_rows, out_grad, kvs, first, heads, earlier):
    big = pl.BlockSpec((TOK, GROUP * DH), lambda i: (0, first + i))
    small = pl.BlockSpec((2, TOK, DH), lambda i: (0, 0, i))
    aliased = len(earlier)
    big_shape = jax.ShapeDtypeStruct(query_rows.shape, jnp.bfloat16)
    small_shape = jax.ShapeDtypeStruct((2, TOK, heads * DH), jnp.bfloat16)
    window = SLOTS * TOK
    pairs = heads * GROUP * TOK * window
    return pl.pallas_call(
        functools.partial(attention_body, aliased),
        grid=(heads,),
        in_specs=[pl.BlockSpec((1, TOK), lambda i: (0, 0)), big, big]
        + [small] * SLOTS
        + [pl.BlockSpec(memory_space=pl.ANY)] * aliased,
        out_specs=[big, big] + [small] * SLOTS,
        out_shape=[big_shape, big_shape] + [small_shape] * SLOTS,
        scratch_shapes=[
            pltpu.VMEM((SLOTS, TOK, TOK), jnp.float32),
            pltpu.VMEM((SLOTS, TOK, TOK), jnp.float32),
            pltpu.VMEM((SLOTS, TOK, GROUP * TOK), jnp.bfloat16),
            pltpu.VMEM((SLOTS, TOK, GROUP * TOK), jnp.bfloat16),
        ],
        input_output_aliases={3 + SLOTS + n: n for n in range(aliased)},
        cost_estimate=pl.CostEstimate(
            flops=24 * pairs * DH,
            bytes_accessed=heads * TOK * DH * 2 * (4 * GROUP + 4 * SLOTS),
            transcendentals=pairs,
        ),
        compiler_params=pltpu.CompilerParams(vmem_limit_bytes=48 * 2**20),
    )(lo, query_rows, out_grad, *kvs, *earlier)


def moved(value, steps, count):
    return lax.ppermute(
        value, AXES, [(i, i + steps) for i in range(count) if 0 <= i + steps < count]
    )


def swapped(value, count):
    return lax.ppermute(value, AXES, [(i, i ^ 1) for i in range(count)])


def on_device(query_rows, key_rows, value_rows, out_grad, doc_lengths):
    count = lax.axis_size(AXES)
    me = lax.axis_index(AXES)
    even = (me % 2) == 0
    ends = jnp.cumsum(doc_lengths, dtype=jnp.int32)
    position = me * TOK + jnp.arange(TOK, dtype=jnp.int32)
    starts = jnp.max(jnp.where(ends[:, None] <= position[None, :], ends[:, None], 0), axis=0)
    lo = (starts - me * TOK)[None, :]
    heads = KVH // CHUNKS
    width = heads * DH
    windows = []
    for c in range(CHUNKS):
        cols = slice(c * width, (c + 1) * width)
        own = jnp.stack([key_rows[:, cols], value_rows[:, cols]])
        two = moved(own, 2, count)
        four = moved(two, 2, count)
        one = swapped(jnp.where(even, own, two), count)
        three = swapped(jnp.where(even, two, four), count)
        windows.append([own, one, two, three, four])
    earlier = []
    grads = []
    for c in range(CHUNKS):
        got = attend(lo, query_rows, out_grad, windows[c], c * heads, heads, earlier)
        earlier = list(got[:2])
        p0, p1, p2, p3, p4 = got[2:]
        f32 = jnp.float32
        y3 = swapped(p3, count).astype(f32)
        y1 = swapped(p1, count).astype(f32)
        zero = jnp.zeros_like(y1)
        s4 = (p4.astype(f32) + jnp.where(even, zero, y3)).astype(jnp.bfloat16)
        z4 = moved(s4, -2, count).astype(f32)
        s2 = (p2.astype(f32) + jnp.where(even, y3, y1) + z4).astype(jnp.bfloat16)
        z2 = moved(s2, -2, count).astype(f32)
        total = p0.astype(f32) + jnp.where(even, y1, zero) + z2
        grads.append(total.astype(jnp.bfloat16))
    grad_key = jnp.concatenate([part[0] for part in grads], axis=1)
    grad_value = jnp.concatenate([part[1] for part in grads], axis=1)
    return (earlier[0], earlier[1], grad_key, grad_value)


def solution(mesh):
    rows = P(AXES, None)
    return jax.shard_map(
        on_device,
        mesh=mesh,
        in_specs=(rows, rows, rows, rows, P()),
        out_specs=(rows, rows, rows, rows),
        check_vma=False,
    )
```

time: 1060 us -> 221 us (0.21); the launches traced: 1040 us -> 221 us
  matrix products: 279 us -> 0 us
  other arithmetic: 253 us -> 4.63 us
  waiting for transfers between devices: 268 us -> 58.2 us
  local copies, waits for them, and re-layouts: 161 us -> 1.44 us
  Pallas kernels: 0 us -> 84.9 us
    dot_general x240 -> x0, matrix products: 279 us -> none  [the longest x40 64.7 us: dweight_piece(): jnp.einsum('tgd,wd->gtw', grad_group, value_piece, preferred_element_type...]
    ppermute x8 -> x16, waiting for transfers between devices: 268 us -> 58.2 us  [the longest x8 48 us: moved(): lax.ppermute(value, AXES, [(i, i + steps) for i in range(count) if 0 <= i...]
    sub x16 -> x1, other arithmetic: 206 us -> 0.01 us  [on_device(): lo = (starts - me * TOK)[None, :]]
    pallas_call x0 -> x2, Pallas kernels: none -> 84.9 us  [attend(): pl.pallas_call(functools.partial(attention_body, aliased), grid=(heads,),...]
    while x40 -> x0, local copies, waits for them, and re-layouts: 63 us -> none
    dynamic_slice x32 -> x0, local copies, waits for them, and re-layouts: 33 us -> none  [the longest x16 23.4 us: one_group(): lax.dynamic_slice_in_dim(out_grad, group_index * group_cols, group_cols, 1)]
    slice x19 -> x0, local copies, waits for them, and re-layouts: 31.9 us -> none  [the longest x8 15.8 us: one_group(): key_group = lax.dynamic_slice_in_dim(window[0], group_index * DH, DH, 1)]
    convert_element_type x8 -> x6, other arithmetic: 30.9 us -> 1.33 us  [the longest x2 0.56 us: on_device(): s2 = (p2.astype(f32) + jnp.where(even, y3, y1) + z4).astype(jnp.bfloat16)]
  transfers between devices with their start and end apart: 8 -> 16, of which waited for: 8 -> 7; matrix products, arithmetic and copies ran while one was open for 0% -> 1% of each run, Pallas kernels for 0% -> 38%
where the time goes in v1:
time: 221 us
  Pallas kernels  84.9 us (38%)
  starting transfers between devices  70.9 us (32%)
  waiting for transfers between devices  58.2 us (26%)
  other arithmetic  4.63 us (2%)
    pallas_call x2, Pallas kernels, attend(): pl.pallas_call(functools.partial(attention_body, aliased), grid=(heads,),...  84.9 us
    ppermute x8, starting transfers between devices, moved(): lax.ppermute(value, AXES, [(i, i + steps) for i in range(count) if 0 <= i...  58.7 us
    ppermute x8, waiting for transfers between devices, moved(): lax.ppermute(value, AXES, [(i, i + steps) for i in range(count) if 0 <= i...  48 us
    ppermute x8, starting transfers between devices, swapped(): return lax.ppermute(value, AXES, [(i, i ^ 1) for i in range(count)])  12.1 us
    ppermute x8, waiting for transfers between devices, swapped(): return lax.ppermute(value, AXES, [(i, i ^ 1) for i in range(count)])  10.2 us
  transfers between devices with their start and end apart: 16, of which 7 were waited for; matrix products, arithmetic and copies ran while one was open for 1% of the time, Pallas kernels for 38%

profile of v1, /device:TPU:1, one launch (start us, length us, event | category | flops | bytes accessed | tf_op | source)
XLA Modules:
  0.0 220.9 jit_solution(11168749726117690951)
XLA Ops:
  0.6 1.3 slice_bitcast_fusion.4
  1.9 0.0 copy-start
  1.9 0.1 pad_maximum_fusion.1.refs_0_
  2.0 4.4 %collective-permute-start.4 = (bf16[2,256,512]{2,1,0:T(8,128)(2,1)S(1)}, bf16[2,256,512]{2,1,0:T(8,128)(2,1)S(1)}, u32[]{:S(2)}, u32[]{:S(2)}) collective-permute-start(bf16[2,256,512]{2,1,0:T(8,128)(2,1)S(1)} %pad_maximum_fusion.1.refs_0_), channel_id=1, source_target_pairs={{0,2},{1,3},{2,4},{3,5},{4,6},{5,7},{6,8},{7,9},{8,10},{9,11},{10,... | collective-permute-start | bytes 1572872 | tf_op jit(solution)/shard_map/ppermute | solution.py:122
  6.4 0.1 pad_maximum_fusion.refs_0_
  6.4 3.5 %collective-permute-start = (bf16[2,256,512]{2,1,0:T(8,128)(2,1)S(1)}, bf16[2,256,512]{2,1,0:T(8,128)(2,1)S(1)}, u32[]{:S(2)}, u32[]{:S(2)}) collective-permute-start(bf16[2,256,512]{2,1,0:T(8,128)(2,1)S(1)} %pad_maximum_fusion.refs_0_), channel_id=1, source_target_pairs={{0,2},{1,3},{2,4},{3,5},{4,6},{5,7},{6,8},{7,9},{8,10},{9,11},{10,... | collective-permute-start | bytes 1572872 | tf_op jit(solution)/shard_map/ppermute | solution.py:122
  10.0 8.4 %collective-permute-done.4.refs_2_ = bf16[2,256,512]{2,1,0:T(8,128)(2,1)S(1)} collective-permute-done((bf16[2,256,512]{2,1,0:T(8,128)(2,1)S(1)}, bf16[2,256,512]{2,1,0:T(8,128)(2,1)S(1)}, u32[]{:S(2)}, u32[]{:S(2)}) %collective-permute-start.4) | collective-permute-done | bytes 524320 | tf_op jit(solution)/shard_map/ppermute | solution.py:122
  18.3 2.7 %collective-permute-start.6 = (bf16[2,256,512]{2,1,0:T(8,128)(2,1)S(1)}, bf16[2,256,512]{2,1,0:T(8,128)(2,1)S(1)}, u32[]{:S(2)}, u32[]{:S(2)}) collective-permute-start(bf16[2,256,512]{2,1,0:T(8,128)(2,1)S(1)} %collective-permute-done.4.refs_2_), channel_id=1, source_target_pairs={{0,2},{1,3},{2,4},{3,5},{4,6},{5,7},{6,8},{7,9},{8,10},{9,11},{10,... | collective-permute-start | bytes 1572872 | tf_op jit(solution)/shard_map/ppermute | solution.py:122
  21.1 0.1 copy.13
  21.2 0.1 reduce-window.8
  21.3 0.1 reduce
  21.4 6.8 %collective-permute-done.refs_2_ = bf16[2,256,512]{2,1,0:T(8,128)(2,1)S(1)} collective-permute-done((bf16[2,256,512]{2,1,0:T(8,128)(2,1)S(1)}, bf16[2,256,512]{2,1,0:T(8,128)(2,1)S(1)}, u32[]{:S(2)}, u32[]{:S(2)}) %collective-permute-start) | collective-permute-done | bytes 524320 | tf_op jit(solution)/shard_map/ppermute | solution.py:122
  28.2 4.1 %collective-permute-start.2 = (bf16[2,256,512]{2,1,0:T(8,128)(2,1)S(1)}, bf16[2,256,512]{2,1,0:T(8,128)(2,1)S(1)}, u32[]{:S(2)}, u32[]{:S(2)}) collective-permute-start(bf16[2,256,512]{2,1,0:T(8,128)(2,1)S(1)} %collective-permute-done.refs_2_), channel_id=1, source_target_pairs={{0,2},{1,3},{2,4},{3,5},{4,6},{5,7},{6,8},{7,9},{8,10},{9,11},{10,... | collective-permute-start | bytes 1572872 | tf_op jit(solution)/shard_map/ppermute | solution.py:122
  32.3 7.1 %collective-permute-done.6.refs_4_ = bf16[2,256,512]{2,1,0:T(8,128)(2,1)S(1)} collective-permute-done((bf16[2,256,512]{2,1,0:T(8,128)(2,1)S(1)}, bf16[2,256,512]{2,1,0:T(8,128)(2,1)S(1)}, u32[]{:S(2)}, u32[]{:S(2)}) %collective-permute-start.6) | collective-permute-done | bytes 524320 | tf_op jit(solution)/shard_map/ppermute | solution.py:122
  39.4 1.1 broadcast_select_fusion
  40.5 2.8 %collective-permute-start.5 = (bf16[2,256,512]{2,1,0:T(8,128)(2,1)S(1)}, bf16[2,256,512]{2,1,0:T(8,128)(2,1)S(1)}, u32[]{:S(2)}, u32[]{:S(2)}) collective-permute-start(bf16[2,256,512]{2,1,0:T(8,128)(2,1)S(1)} %get-tuple-element.37), channel_id=1, source_target_pairs={{0,1},{1,0},{2,3},{3,2},{4,5},{5,4},{6,7},{7,6},{8,9},{9,8},{10,11... | collective-permute-start | bytes 1572872 | tf_op jit(solution)/shard_map/ppermute | solution.py:128
  43.3 0.2 collective-permute-start.7
  43.5 0.1 select_reduce_fusion
  43.6 7.0 %collective-permute-done.2.refs_4_ = bf16[2,256,512]{2,1,0:T(8,128)(2,1)S(1)} collective-permute-done((bf16[2,256,512]{2,1,0:T(8,128)(2,1)S(1)}, bf16[2,256,512]{2,1,0:T(8,128)(2,1)S(1)}, u32[]{:S(2)}, u32[]{:S(2)}) %collective-permute-start.2) | collective-permute-done | bytes 524320 | tf_op jit(solution)/shard_map/ppermute | solution.py:122
  50.6 0.1 broadcast_select_fusion.2
  50.7 2.8 %collective-permute-start.1 = (bf16[2,256,512]{2,1,0:T(8,128)(2,1)S(1)}, bf16[2,256,512]{2,1,0:T(8,128)(2,1)S(1)}, u32[]{:S(2)}, u32[]{:S(2)}) collective-permute-start(bf16[2,256,512]{2,1,0:T(8,128)(2,1)S(1)} %get-tuple-element.43), channel_id=1, source_target_pairs={{0,1},{1,0},{2,3},{3,2},{4,5},{5,4},{6,7},{7,6},{8,9},{9,8},{10,11... | collective-permute-start | bytes 1572872 | tf_op jit(solution)/shard_map/ppermute | solution.py:128
  53.6 0.2 collective-permute-start.3
  53.8 0.0 collective-permute-done.5.refs_1_
  53.8 10.2 %collective-permute-done.7.refs_3_ = bf16[2,256,512]{2,1,0:T(8,128)(2,1)S(1)} collective-permute-done((bf16[2,256,512]{2,1,0:T(8,128)(2,1)S(1)}, bf16[2,256,512]{2,1,0:T(8,128)(2,1)S(1)}, u32[]{:S(2)}, u32[]{:S(2)}) %collective-permute-start.7) | collective-permute-done | bytes 524320 | tf_op jit(solution)/shard_map/ppermute | solution.py:128
  64.0 42.4 %shard_map.84 = (bf16[256,6144]{1,0:T(8,128)(2,1)}, bf16[256,6144]{1,0:T(8,128)(2,1)}, bf16[2,256,512]{2,1,0:T(8,128)(2,1)S(1)}, bf16[2,256,512]{2,1,0:T(8,128)(...) custom-call(s32[1,256]{1,0:T(1,128)S(1)} %bitcast.18, ...), custom_call_target="tpu_custom_call" | custom-call | flops 24159191040 | bytes 11534336 | tf_op jit(solution)/shard_map/pallas_call | solution.py:97
  106.4 2.8 %collective-permute-start.9 = (bf16[2,256,512]{2,1,0:T(8,128)(2,1)S(1)}, bf16[2,256,512]{2,1,0:T(8,128)(2,1)S(1)}, u32[]{:S(2)}, u32[]{:S(2)}) collective-permute-start(bf16[2,256,512]{2,1,0:T(8,128)(2,1)S(1)} %get-tuple-element.25), channel_id=1, source_target_pairs={{0,1},{1,0},{2,3},{3,2},{4,5},{5,4},{6,7},{7,6},{8,9},{9,8},{10,11... | collective-permute-start | bytes 1572872 | tf_op jit(solution)/shard_map/ppermute | solution.py:128
  109.2 42.5 %shard_map.85 = (bf16[256,6144]{1,0:T(8,128)(2,1)}, bf16[256,6144]{1,0:T(8,128)(2,1)}, bf16[2,256,512]{2,1,0:T(8,128)(2,1)S(1)}, bf16[2,256,512]{2,1,0:T(8,128)(...) custom-call(s32[1,256]{1,0:T(1,128)S(1)} %bitcast.19, ...), custom_call_target="tpu_custom_call", output_to_operand_aliasing={{0}: (8, {}), {1}: (9, {})} | custom-call | flops 24159191040 | bytes 11534336 | tf_op jit(solution)/shard_map/pallas_call | solution.py:97
  151.6 0.2 collective-permute-start.13
  151.9 2.7 %collective-permute-start.8 = (bf16[2,256,512]{2,1,0:T(8,128)(2,1)S(1)}, bf16[2,256,512]{2,1,0:T(8,128)(2,1)S(1)}, u32[]{:S(2)}, u32[]{:S(2)}) collective-permute-start(bf16[2,256,512]{2,1,0:T(8,128)(2,1)S(1)} %get-tuple-element.23), channel_id=1, source_target_pairs={{0,1},{1,0},{2,3},{3,2},{4,5},{5,4},{6,7},{7,6},{8,9},{9,8},{10,11... | collective-permute-start | bytes 1572872 | tf_op jit(solution)/shard_map/ppermute | solution.py:128
  154.6 0.0 collective-permute-done.9
  154.6 0.2 fusion.7
  154.8 16.2 %collective-permute-start.10 = (bf16[2,256,512]{2,1,0:T(8,128)(2,1)S(1)}, bf16[2,256,512]{2,1,0:T(8,128)(2,1)S(1)}, u32[]{:S(2)}, u32[]{:S(2)}) collective-permute-start(bf16[2,256,512]{2,1,0:T(8,128)(2,1)S(1)} %fusion.7), channel_id=1, source_target_pairs={{2,0},{3,1},{4,2},{5,3},{6,4},{7,5},{8,6},{9,7},{10,8},{11,9},{12,... | collective-permute-start | bytes 1572872 | tf_op jit(solution)/shard_map/ppermute | solution.py:122
  171.0 0.3 collective-permute-start.12
  171.3 0.0 collective-permute-done.13
  171.3 0.2 fusion.15
  171.5 12.4 %collective-permute-start.14 = (bf16[2,256,512]{2,1,0:T(8,128)(2,1)S(1)}, bf16[2,256,512]{2,1,0:T(8,128)(2,1)S(1)}, u32[]{:S(2)}, u32[]{:S(2)}) collective-permute-start(bf16[2,256,512]{2,1,0:T(8,128)(2,1)S(1)} %fusion.15), channel_id=1, source_target_pairs={{2,0},{3,1},{4,2},{5,3},{6,4},{7,5},{8,6},{9,7},{10,8},{11,9},{12,... | collective-permute-start | bytes 1572872 | tf_op jit(solution)/shard_map/ppermute | solution.py:122
  183.8 0.0 collective-permute-done.8
  183.9 0.3 fusion.5
  184.1 9.0 %collective-permute-start.11 = (bf16[2,256,512]{2,1,0:T(8,128)(2,1)S(1)}, bf16[2,256,512]{2,1,0:T(8,128)(2,1)S(1)}, u32[]{:S(2)}, u32[]{:S(2)}) collective-permute-start(bf16[2,256,512]{2,1,0:T(8,128)(2,1)S(1)} %fusion.5), channel_id=1, source_target_pairs={{2,0},{3,1},{4,2},{5,3},{6,4},{7,5},{8,6},{9,7},{10,8},{11,9},{12,... | collective-permute-start | bytes 1572872 | tf_op jit(solution)/shard_map/ppermute | solution.py:122
  193.2 0.0 collective-permute-done.12
  193.2 0.3 fusion.13
  193.5 6.4 %collective-permute-start.15 = (bf16[2,256,512]{2,1,0:T(8,128)(2,1)S(1)}, bf16[2,256,512]{2,1,0:T(8,128)(2,1)S(1)}, u32[]{:S(2)}, u32[]{:S(2)}) collective-permute-start(bf16[2,256,512]{2,1,0:T(8,128)(2,1)S(1)} %fusion.13), channel_id=1, source_target_pairs={{2,0},{3,1},{4,2},{5,3},{6,4},{7,5},{8,6},{9,7},{10,8},{11,9},{12,... | collective-permute-start | bytes 1572872 | tf_op jit(solution)/shard_map/ppermute | solution.py:122
  199.9 13.4 %collective-permute-done.11 = bf16[2,256,512]{2,1,0:T(8,128)(2,1)S(1)} collective-permute-done((bf16[2,256,512]{2,1,0:T(8,128)(2,1)S(1)}, bf16[2,256,512]{2,1,0:T(8,128)(2,1)S(1)}, u32[]{:S(2)}, u32[]{:S(2)}) %collective-permute-start.11) | collective-permute-done | bytes 524320 | tf_op jit(solution)/shard_map/ppermute | solution.py:122
  213.3 0.2 fusion.2
  213.6 5.3 %collective-permute-done.15 = bf16[2,256,512]{2,1,0:T(8,128)(2,1)S(1)} collective-permute-done((bf16[2,256,512]{2,1,0:T(8,128)(2,1)S(1)}, bf16[2,256,512]{2,1,0:T(8,128)(2,1)S(1)}, u32[]{:S(2)}, u32[]{:S(2)}) %collective-permute-start.15) | collective-permute-done | bytes 524320 | tf_op jit(solution)/shard_map/ppermute | solution.py:122
  218.9 0.2 fusion.10
  219.2 0.9 pad_maximum_fusion.3
  220.0 0.9 pad_maximum_fusion.2
  (11 shorter events, 0.1 us)
Async XLA Ops:
  0.6 20.4 %copy-start.1 = (s32[64]{0:T(128)S(1)}, s32[64]{0:T(128)}, u32[]{:S(2)}) copy-start(s32[64]{0:T(128)} %param.9) | copy-start | bytes 772
  1.9 4.5 %copy-start = (bf16[1,256,512]{2,1,0:T(8,128)(2,1)}, bf16[1,256,512]{2,1,0:T(8,128)(2,1)S(1)}, u32[]{:S(2)}) copy-start(bf16[1,256,512]{2,1,0:T(8,128)(2,1)S(1)} %get-tuple-element.45) | copy-start | bytes 786436
  2.0 16.4 %collective-permute-start.4 = (bf16[2,256,512]{2,1,0:T(8,128)(2,1)S(1)}, bf16[2,256,512]{2,1,0:T(8,128)(2,1)S(1)}, u32[]{:S(2)}, u32[]{:S(2)}) collective-permute-start(bf16[2,256,512]{2,1,0:T(8,128)(2,1)S(1)} %pad_maximum_fusion.1.refs_0_), channel_id=1, source_target_pairs={{0,2},{1,3},{2,4},{3,5},{4,6},{5,7},{6,8},{7,9},{8,10},{9,11},{10,... | collective-permute-start | bytes 1572872 | tf_op jit(solution)/shard_map/ppermute | solution.py:122
  6.4 21.7 %collective-permute-start = (bf16[2,256,512]{2,1,0:T(8,128)(2,1)S(1)}, bf16[2,256,512]{2,1,0:T(8,128)(2,1)S(1)}, u32[]{:S(2)}, u32[]{:S(2)}) collective-permute-start(bf16[2,256,512]{2,1,0:T(8,128)(2,1)S(1)} %pad_maximum_fusion.refs_0_), channel_id=1, source_target_pairs={{0,2},{1,3},{2,4},{3,5},{4,6},{5,7},{6,8},{7,9},{8,10},{9,11},{10,... | collective-permute-start | bytes 1572872 | tf_op jit(solution)/shard_map/ppermute | solution.py:122
  18.3 21.1 %collective-permute-start.6 = (bf16[2,256,512]{2,1,0:T(8,128)(2,1)S(1)}, bf16[2,256,512]{2,1,0:T(8,128)(2,1)S(1)}, u32[]{:S(2)}, u32[]{:S(2)}) collective-permute-start(bf16[2,256,512]{2,1,0:T(8,128)(2,1)S(1)} %collective-permute-done.4.refs_2_), channel_id=1, source_target_pairs={{0,2},{1,3},{2,4},{3,5},{4,6},{5,7},{6,8},{7,9},{8,10},{9,11},{10,... | collective-permute-start | bytes 1572872 | tf_op jit(solution)/shard_map/ppermute | solution.py:122
  28.2 22.5 %collective-permute-start.2 = (bf16[2,256,512]{2,1,0:T(8,128)(2,1)S(1)}, bf16[2,256,512]{2,1,0:T(8,128)(2,1)S(1)}, u32[]{:S(2)}, u32[]{:S(2)}) collective-permute-start(bf16[2,256,512]{2,1,0:T(8,128)(2,1)S(1)} %collective-permute-done.refs_2_), channel_id=1, source_target_pairs={{0,2},{1,3},{2,4},{3,5},{4,6},{5,7},{6,8},{7,9},{8,10},{9,11},{10,... | collective-permute-start | bytes 1572872 | tf_op jit(solution)/shard_map/ppermute | solution.py:122
  40.5 13.3 %collective-permute-start.5 = (bf16[2,256,512]{2,1,0:T(8,128)(2,1)S(1)}, bf16[2,256,512]{2,1,0:T(8,128)(2,1)S(1)}, u32[]{:S(2)}, u32[]{:S(2)}) collective-permute-start(bf16[2,256,512]{2,1,0:T(8,128)(2,1)S(1)} %get-tuple-element.37), channel_id=1, source_target_pairs={{0,1},{1,0},{2,3},{3,2},{4,5},{5,4},{6,7},{7,6},{8,9},{9,8},{10,11... | collective-permute-start | bytes 1572872 | tf_op jit(solution)/shard_map/ppermute | solution.py:128
  43.3 20.7 %collective-permute-start.7 = (bf16[2,256,512]{2,1,0:T(8,128)(2,1)S(1)}, bf16[2,256,512]{2,1,0:T(8,128)(2,1)S(1)}, u32[]{:S(2)}, u32[]{:S(2)}) collective-permute-start(bf16[2,256,512]{2,1,0:T(8,128)(2,1)S(1)} %get-tuple-element.36), channel_id=1, source_target_pairs={{0,1},{1,0},{2,3},{3,2},{4,5},{5,4},{6,7},{7,6},{8,9},{9,8},{10,11... | collective-permute-start | bytes 1572872 | tf_op jit(solution)/shard_map/ppermute | solution.py:128
  50.7 58.4 %collective-permute-start.1 = (bf16[2,256,512]{2,1,0:T(8,128)(2,1)S(1)}, bf16[2,256,512]{2,1,0:T(8,128)(2,1)S(1)}, u32[]{:S(2)}, u32[]{:S(2)}) collective-permute-start(bf16[2,256,512]{2,1,0:T(8,128)(2,1)S(1)} %get-tuple-element.43), channel_id=1, source_target_pairs={{0,1},{1,0},{2,3},{3,2},{4,5},{5,4},{6,7},{7,6},{8,9},{9,8},{10,11... | collective-permute-start | bytes 1572872 | tf_op jit(solution)/shard_map/ppermute | solution.py:128
  53.6 55.6 %collective-permute-start.3 = (bf16[2,256,512]{2,1,0:T(8,128)(2,1)S(1)}, bf16[2,256,512]{2,1,0:T(8,128)(2,1)S(1)}, u32[]{:S(2)}, u32[]{:S(2)}) collective-permute-start(bf16[2,256,512]{2,1,0:T(8,128)(2,1)S(1)} %get-tuple-element.42), channel_id=1, source_target_pairs={{0,1},{1,0},{2,3},{3,2},{4,5},{5,4},{6,7},{7,6},{8,9},{9,8},{10,11... | collective-permute-start | bytes 1572872 | tf_op jit(solution)/shard_map/ppermute | solution.py:128
  106.4 48.2 %collective-permute-start.9 = (bf16[2,256,512]{2,1,0:T(8,128)(2,1)S(1)}, bf16[2,256,512]{2,1,0:T(8,128)(2,1)S(1)}, u32[]{:S(2)}, u32[]{:S(2)}) collective-permute-start(bf16[2,256,512]{2,1,0:T(8,128)(2,1)S(1)} %get-tuple-element.25), channel_id=1, source_target_pairs={{0,1},{1,0},{2,3},{3,2},{4,5},{5,4},{6,7},{7,6},{8,9},{9,8},{10,11... | collective-permute-start | bytes 1572872 | tf_op jit(solution)/shard_map/ppermute | solution.py:128
  151.6 19.7 %collective-permute-start.13 = (bf16[2,256,512]{2,1,0:T(8,128)(2,1)S(1)}, bf16[2,256,512]{2,1,0:T(8,128)(2,1)S(1)}, u32[]{:S(2)}, u32[]{:S(2)}) collective-permute-start(bf16[2,256,512]{2,1,0:T(8,128)(2,1)S(1)} %get-tuple-element.30), channel_id=1, source_target_pairs={{0,1},{1,0},{2,3},{3,2},{4,5},{5,4},{6,7},{7,6},{8,9},{9,8},{10,11... | collective-permute-start | bytes 1572872 | tf_op jit(solution)/shard_map/ppermute | solution.py:128
  151.9 32.0 %collective-permute-start.8 = (bf16[2,256,512]{2,1,0:T(8,128)(2,1)S(1)}, bf16[2,256,512]{2,1,0:T(8,128)(2,1)S(1)}, u32[]{:S(2)}, u32[]{:S(2)}) collective-permute-start(bf16[2,256,512]{2,1,0:T(8,128)(2,1)S(1)} %get-tuple-element.23), channel_id=1, source_target_pairs={{0,1},{1,0},{2,3},{3,2},{4,5},{5,4},{6,7},{7,6},{8,9},{9,8},{10,11... | collective-permute-start | bytes 1572872 | tf_op jit(solution)/shard_map/ppermute | solution.py:128
  154.8 29.1 %collective-permute-start.10 = (bf16[2,256,512]{2,1,0:T(8,128)(2,1)S(1)}, bf16[2,256,512]{2,1,0:T(8,128)(2,1)S(1)}, u32[]{:S(2)}, u32[]{:S(2)}) collective-permute-start(bf16[2,256,512]{2,1,0:T(8,128)(2,1)S(1)} %fusion.7), channel_id=1, source_target_pairs={{2,0},{3,1},{4,2},{5,3},{6,4},{7,5},{8,6},{9,7},{10,8},{11,9},{12,... | collective-permute-start | bytes 1572872 | tf_op jit(solution)/shard_map/ppermute | solution.py:122
  171.0 22.2 %collective-permute-start.12 = (bf16[2,256,512]{2,1,0:T(8,128)(2,1)S(1)}, bf16[2,256,512]{2,1,0:T(8,128)(2,1)S(1)}, u32[]{:S(2)}, u32[]{:S(2)}) collective-permute-start(bf16[2,256,512]{2,1,0:T(8,128)(2,1)S(1)} %get-tuple-element.28), channel_id=1, source_target_pairs={{0,1},{1,0},{2,3},{3,2},{4,5},{5,4},{6,7},{7,6},{8,9},{9,8},{10,11... | collective-permute-start | bytes 1572872 | tf_op jit(solution)/shard_map/ppermute | solution.py:128
  171.5 21.7 %collective-permute-start.14 = (bf16[2,256,512]{2,1,0:T(8,128)(2,1)S(1)}, bf16[2,256,512]{2,1,0:T(8,128)(2,1)S(1)}, u32[]{:S(2)}, u32[]{:S(2)}) collective-permute-start(bf16[2,256,512]{2,1,0:T(8,128)(2,1)S(1)} %fusion.15), channel_id=1, source_target_pairs={{2,0},{3,1},{4,2},{5,3},{6,4},{7,5},{8,6},{9,7},{10,8},{11,9},{12,... | collective-permute-start | bytes 1572872 | tf_op jit(solution)/shard_map/ppermute | solution.py:122
  184.1 29.1 %collective-permute-start.11 = (bf16[2,256,512]{2,1,0:T(8,128)(2,1)S(1)}, bf16[2,256,512]{2,1,0:T(8,128)(2,1)S(1)}, u32[]{:S(2)}, u32[]{:S(2)}) collective-permute-start(bf16[2,256,512]{2,1,0:T(8,128)(2,1)S(1)} %fusion.5), channel_id=1, source_target_pairs={{2,0},{3,1},{4,2},{5,3},{6,4},{7,5},{8,6},{9,7},{10,8},{11,9},{12,... | collective-permute-start | bytes 1572872 | tf_op jit(solution)/shard_map/ppermute | solution.py:122
  193.5 25.4 %collective-permute-start.15 = (bf16[2,256,512]{2,1,0:T(8,128)(2,1)S(1)}, bf16[2,256,512]{2,1,0:T(8,128)(2,1)S(1)}, u32[]{:S(2)}, u32[]{:S(2)}) collective-permute-start(bf16[2,256,512]{2,1,0:T(8,128)(2,1)S(1)} %fusion.13), channel_id=1, source_target_pairs={{2,0},{3,1},{4,2},{5,3},{6,4},{7,5},{8,6},{9,7},{10,8},{11,9},{12,... | collective-permute-start | bytes 1572872 | tf_op jit(solution)/shard_map/ppermute | solution.py:122

commit v2 on v1

v2 whole, which is shorter than its diff:
```python
import functools

import jax
import jax.numpy as jnp
from jax import lax
from jax.experimental import pallas as pl
from jax.experimental.pallas import tpu as pltpu
from jax.sharding import PartitionSpec as P

KVH = 8
GROUP = 6
DH = 128
REACH = 4
SLOTS = REACH + 1
TOK = 256
AXES = ("inner", "outer")
SCALE = DH ** (-0.5)
LOG2E = 1.4426950408889634
MASKED = -1e30
WIDE = 3
SPLIT = 2
PRE = False
TIE = True
NN = (((1,), (0,)), ((), ()))
NT = (((1,), (1,)), ((), ()))


def mm(left, right, dims=NN):
    return lax.dot_general(left, right, dims, preferred_element_type=jnp.float32)


def attention_body(aliased, lo_ref, q_ref, g_ref, *refs):
    kv = refs[:SLOTS]
    refs = refs[SLOTS + aliased :]
    out_ref, dq_ref = refs[:2]
    dkv = refs[2 : 2 + SLOTS]
    bias_ref, e_refs, w_ref, ds_ref, kt_ref, vt_ref, qt_ref, gt_ref = refs[2 + SLOTS :]

    @pl.when(pl.program_id(0) == 0)
    def _():
        lo = lo_ref[...]
        qpos = lax.broadcasted_iota(jnp.int32, (TOK, TOK), 1)
        kpos = lax.broadcasted_iota(jnp.int32, (TOK, TOK), 0)
        for d in range(SLOTS):
            k = kpos - d * TOK
            ok = (k >= lo) & (k <= qpos)
            bias_ref[d * TOK : (d + 1) * TOK] = jnp.where(ok, 0.0, MASKED)

    for d in range(SLOTS):
        rows = slice(d * TOK, (d + 1) * TOK)
        kt_ref[:, rows] = kv[d][0].T
        vt_ref[:, rows] = kv[d][1].T
    for h in range(GROUP):
        cols = slice(h * DH, (h + 1) * DH)
        qc = slice(h * TOK, (h + 1) * TOK)
        qt_ref[:, qc] = q_ref[:, cols].T
        gt_ref[:, qc] = g_ref[:, cols].T
    for first in range(0, GROUP, WIDE):
        wide = slice(first * TOK, (first + WIDE) * TOK)
        for h in range(first, first + WIDE):
            e_ref = e_refs.at[h % 2]
            qc = slice(h * TOK, (h + 1) * TOK)
            qt = qt_ref[:, qc]
            peaks, sums = [], []
            for d in range(SLOTS):
                rows = slice(d * TOK, (d + 1) * TOK)
                t = mm(kv[d][0], qt) * (SCALE * LOG2E) + bias_ref[rows]
                peak = jnp.max(t, axis=0, keepdims=True)
                e = jnp.exp2(t - peak)
                sums.append(jnp.sum(e, axis=0, keepdims=True))
                peaks.append(peak)
                e_ref[rows] = e
            top = functools.reduce(jnp.maximum, peaks)
            factors = [jnp.exp2(peak - top) for peak in peaks]
            inverse = 1.0 / functools.reduce(
                jnp.add, [part * factor for part, factor in zip(sums, factors)]
            )
            for d, factor in enumerate(factors):
                rows = slice(d * TOK, (d + 1) * TOK)
                w_ref[rows, qc] = (e_ref[rows] * (factor * inverse)).astype(jnp.bfloat16)
        out_wide = mm(vt_ref[...], w_ref[:, wide])
        for h in range(first, first + WIDE):
            cols = slice(h * DH, (h + 1) * DH)
            qc = slice(h * TOK, (h + 1) * TOK)
            gt = gt_ref[:, qc]
            out = out_wide[:, (h - first) * TOK : (h - first + 1) * TOK]
            out_ref[:, cols] = out.T.astype(jnp.bfloat16)
            delta = jnp.sum(out * gt.astype(jnp.float32), axis=0, keepdims=True)
            for d in range(SLOTS):
                rows = slice(d * TOK, (d + 1) * TOK)
                dp = mm(kv[d][1], gt)
                weights = w_ref[rows, qc].astype(jnp.float32)
                ds_ref[rows, qc] = (weights * (dp - delta)).astype(jnp.bfloat16)
        dq_wide = mm(kt_ref[...], ds_ref[:, wide]) * SCALE
        for n in range(WIDE):
            cols = slice((first + n) * DH, (first + n + 1) * DH)
            dq_ref[:, cols] = dq_wide[:, n * TOK : (n + 1) * TOK].T.astype(jnp.bfloat16)
    qs = jnp.concatenate([q_ref[:, h * DH : (h + 1) * DH] for h in range(GROUP)], axis=0)
    gs = jnp.concatenate([g_ref[:, h * DH : (h + 1) * DH] for h in range(GROUP)], axis=0)
    for d in range(SLOTS):
        rows = slice(d * TOK, (d + 1) * TOK)
        dkv[d][0] = (mm(ds_ref[rows], qs) * SCALE).astype(jnp.bfloat16)
        dkv[d][1] = mm(w_ref[rows], gs).astype(jnp.bfloat16)


def attend(lo, query_rows, out_grad, kvs, first, skip, heads, earlier):
    big = pl.BlockSpec((TOK, GROUP * DH), lambda i: (0, first + i))
    small = pl.BlockSpec((2, TOK, DH), lambda i: (0, 0, skip + i))
    part = pl.BlockSpec((2, TOK, DH), lambda i: (0, 0, i))
    aliased = len(earlier)
    big_shape = jax.ShapeDtypeStruct(query_rows.shape, jnp.bfloat16)
    small_shape = jax.ShapeDtypeStruct((2, TOK, heads * DH), jnp.bfloat16)
    window = SLOTS * TOK
    pairs = heads * GROUP * TOK * window
    return pl.pallas_call(
        functools.partial(attention_body, aliased),
        grid=(heads,),
        in_specs=[pl.BlockSpec((1, TOK), lambda i: (0, 0)), big, big]
        + [small] * SLOTS
        + [pl.BlockSpec(memory_space=pl.ANY)] * aliased,
        out_specs=[big, big] + [part] * SLOTS,
        out_shape=[big_shape, big_shape] + [small_shape] * SLOTS,
        scratch_shapes=[
            pltpu.VMEM((window, TOK), jnp.float32),
            pltpu.VMEM((2, window, TOK), jnp.float32),
            pltpu.VMEM((window, GROUP * TOK), jnp.bfloat16),
            pltpu.VMEM((window, GROUP * TOK), jnp.bfloat16),
            pltpu.VMEM((DH, window), jnp.bfloat16),
            pltpu.VMEM((DH, window), jnp.bfloat16),
            pltpu.VMEM((DH, GROUP * TOK), jnp.bfloat16),
            pltpu.VMEM((DH, GROUP * TOK), jnp.bfloat16),
        ],
        input_output_aliases={3 + SLOTS + n: n for n in range(aliased)},
        cost_estimate=pl.CostEstimate(
            flops=24 * pairs * DH,
            bytes_accessed=heads * TOK * DH * 2 * (4 * GROUP + 4 * SLOTS),
            transcendentals=pairs,
        ),
        compiler_params=pltpu.CompilerParams(vmem_limit_bytes=48 * 2**20),
    )(lo, query_rows, out_grad, *kvs, *earlier)


def moved(value, steps, count):
    return lax.ppermute(
        value, AXES, [(i, i + steps) for i in range(count) if 0 <= i + steps < count]
    )


def swapped(value, count):
    return lax.ppermute(value, AXES, [(i, i ^ 1) for i in range(count)])


def after(value, *earlier):
    return lax.optimization_barrier((value, *earlier))[0]


def on_device(query_rows, key_rows, value_rows, out_grad, doc_lengths):
    count = lax.axis_size(AXES)
    me = lax.axis_index(AXES)
    even = (me % 2) == 0
    ends = jnp.cumsum(doc_lengths, dtype=jnp.int32)
    position = me * TOK + jnp.arange(TOK, dtype=jnp.int32)
    starts = jnp.max(jnp.where(ends[:, None] <= position[None, :], ends[:, None], 0), axis=0)
    lo = (starts - me * TOK)[None, :]
    f32, bf16 = jnp.float32, jnp.bfloat16
    half = KVH // 2
    width = half * DH
    own0 = jnp.stack([key_rows[:, :width], value_rows[:, :width]])
    own1 = jnp.stack([key_rows[:, width:], value_rows[:, width:]])

    def call(window, chunk, skip, heads, earlier):
        got = attend(
            lo, query_rows, out_grad, window, chunk * half + skip, skip, heads, earlier
        )
        return list(got[:2]), got[2:]

    two0 = moved(own0, 2, count)
    one0 = swapped(jnp.where(even, own0, two0), count)
    four0 = moved(two0, 2, count)
    three0 = swapped(jnp.where(even, two0, four0), count)
    two1 = moved(after(own1, two0), 2, count)
    window = [own0, one0, two0, three0, four0]
    if PRE:
        three0, two1 = lax.optimization_barrier((three0, two1))
        window[3] = three0
    sendable = after(two1, three0)
    four1 = moved(sendable, 2, count)
    one1 = swapped(jnp.where(even, own1, sendable), count)
    big, a = call(window, 0, 0, SPLIT, [])
    three1 = swapped(jnp.where(even, two1, four1), count)
    if TIE:
        tied = lax.optimization_barrier((big, four1, one1))
        big, four1, one1 = tied
    big, b = call(window, 0, SPLIT, half - SPLIT, big)
    p0, p1, p2, p3, p4 = [jnp.concatenate(pair, axis=2) for pair in zip(a, b)]
    y3 = swapped(p3, count)
    window = [own1, one1, two1, three1, four1]
    big, a = call(window, 1, 0, SPLIT, big)
    if TIE:
        big, y3 = lax.optimization_barrier((big, y3))
    y1 = swapped(after(p1, y3), count).astype(f32)
    y3 = y3.astype(f32)
    s4 = (p4.astype(f32) + jnp.where(even, 0.0, y3)).astype(bf16)
    z4 = moved(s4, -2, count).astype(f32)
    big, b = call(window, 1, SPLIT, half - SPLIT, big)
    s2 = (p2.astype(f32) + jnp.where(even, y3, y1) + z4).astype(bf16)
    q0, q1, q2, q3, q4 = [jnp.concatenate(pair, axis=2) for pair in zip(a, b)]
    x3 = swapped(q3, count)
    z2 = moved(after(s2, big[0]), -2, count).astype(f32)
    total0 = p0.astype(f32) + jnp.where(even, y1, 0.0) + z2
    x1 = swapped(after(q1, x3), count).astype(f32)
    x3 = x3.astype(f32)
    s4 = (q4.astype(f32) + jnp.where(even, 0.0, x3)).astype(bf16)
    z4 = moved(s4, -2, count).astype(f32)
    s2 = (q2.astype(f32) + jnp.where(even, x3, x1) + z4).astype(bf16)
    z2 = moved(s2, -2, count).astype(f32)
    total1 = q0.astype(f32) + jnp.where(even, x1, 0.0) + z2
    grads = jnp.concatenate([total0.astype(bf16), total1.astype(bf16)], axis=2)
    return (big[0], big[1], grads[0], grads[1])


def solution(mesh):
    rows = P(AXES, None)
    return jax.shard_map(
        on_device,
        mesh=mesh,
        in_specs=(rows, rows, rows, rows, P()),
        out_specs=(rows, rows, rows, rows),
        check_vma=False,
    )
```

time: 221 us -> 195 us (0.88)
  Pallas kernels: 84.9 us -> 66.4 us
  waiting for transfers between devices: 58.2 us -> 52.1 us
    pallas_call x2 -> x4, Pallas kernels: 84.9 us -> 66.4 us  [attend(): pl.pallas_call(functools.partial(attention_body, aliased), grid=(heads,),...]
    ppermute x8, waiting for transfers between devices: 48 us -> 39.8 us  [moved(): lax.ppermute(value, AXES, [(i, i + steps) for i in range(count) if 0 <= i...]
    ppermute x8, starting transfers between devices: 58.7 us -> 53.8 us  [moved(): lax.ppermute(value, AXES, [(i, i + steps) for i in range(count) if 0 <= i...]
    ppermute x8, starting transfers between devices: 12.1 us -> 15.4 us  [swapped(): return lax.ppermute(value, AXES, [(i, i ^ 1) for i in range(count)])]
  transfers between devices with their start and end apart: 16 -> 16, of which waited for: 7 -> 7; matrix products, arithmetic and copies ran while one was open for 1% -> 2% of each run, Pallas kernels for 38% -> 25%
where the time goes in v2:
time: 195 us
  starting transfers between devices  69.2 us (35%)
  Pallas kernels  66.4 us (34%)
  waiting for transfers between devices  52.1 us (27%)
  other arithmetic  5.11 us (3%)
    pallas_call x4, Pallas kernels, attend(): pl.pallas_call(functools.partial(attention_body, aliased), grid=(heads,),...  66.4 us
    ppermute x8, starting transfers between devices, moved(): lax.ppermute(value, AXES, [(i, i + steps) for i in range(count) if 0 <= i...  53.8 us
    ppermute x8, waiting for transfers between devices, moved(): lax.ppermute(value, AXES, [(i, i + steps) for i in range(count) if 0 <= i...  39.8 us
    ppermute x8, starting transfers between devices, swapped(): return lax.ppermute(value, AXES, [(i, i ^ 1) for i in range(count)])  15.4 us
    ppermute x8, waiting for transfers between devices, swapped(): return lax.ppermute(value, AXES, [(i, i ^ 1) for i in range(count)])  12.3 us
  transfers between devices with their start and end apart: 16, of which 7 were waited for; matrix products, arithmetic and copies ran while one was open for 2% of the time, Pallas kernels for 25%

profile of v2, /device:TPU:1, one launch (start us, length us, event | category | flops | bytes accessed | tf_op | source)
XLA Modules:
  0.0 195.1 jit_solution(798050785352550411)
XLA Ops:
  0.6 1.3 slice_bitcast_fusion
  1.9 0.0 copy-start
  1.9 0.1 pad_maximum_fusion.2.refs_0_
  2.0 4.4 %collective-permute-start = (bf16[2,256,512]{2,1,0:T(8,128)(2,1)S(1)}, bf16[2,256,512]{2,1,0:T(8,128)(2,1)S(1)}, u32[]{:S(2)}, u32[]{:S(2)}) collective-permute-start(bf16[2,256,512]{2,1,0:T(8,128)(2,1)S(1)} %pad_maximum_fusion.2.refs_0_), channel_id=1, source_target_pairs={{0,2},{1,3},{2,4},{3,5},{4,6},{5,7},{6,8},{7,9},{8,10},{9,11},{10,... | collective-permute-start | bytes 1572872 | tf_op jit(solution)/shard_map/ppermute | solution.py:144
  6.4 12.0 %collective-permute-done.refs_2_ = bf16[2,256,512]{2,1,0:T(8,128)(2,1)S(1)} collective-permute-done((bf16[2,256,512]{2,1,0:T(8,128)(2,1)S(1)}, bf16[2,256,512]{2,1,0:T(8,128)(2,1)S(1)}, u32[]{:S(2)}, u32[]{:S(2)}) %collective-permute-start) | collective-permute-done | bytes 524320 | tf_op jit(solution)/shard_map/ppermute | solution.py:144
  18.3 2.7 %collective-permute-start.2 = (bf16[2,256,512]{2,1,0:T(8,128)(2,1)S(1)}, bf16[2,256,512]{2,1,0:T(8,128)(2,1)S(1)}, u32[]{:S(2)}, u32[]{:S(2)}) collective-permute-start(bf16[2,256,512]{2,1,0:T(8,128)(2,1)S(1)} %collective-permute-done.refs_2_), channel_id=1, source_target_pairs={{0,2},{1,3},{2,4},{3,5},{4,6},{5,7},{6,8},{7,9},{8,10},{9,11},{10,... | collective-permute-start | bytes 1572872 | tf_op jit(solution)/shard_map/ppermute | solution.py:144
  21.1 0.1 pad_maximum_fusion.1.refs_0_
  21.1 3.5 %collective-permute-start.4 = (bf16[2,256,512]{2,1,0:T(8,128)(2,1)S(1)}, bf16[2,256,512]{2,1,0:T(8,128)(2,1)S(1)}, u32[]{:S(2)}, u32[]{:S(2)}) collective-permute-start(bf16[2,256,512]{2,1,0:T(8,128)(2,1)S(1)} %pad_maximum_fusion.1.refs_0_), channel_id=1, source_target_pairs={{0,2},{1,3},{2,4},{3,5},{4,6},{5,7},{6,8},{7,9},{8,10},{9,11},{10,... | collective-permute-start | bytes 1572872 | tf_op jit(solution)/shard_map/ppermute | solution.py:144
  24.7 9.2 %collective-permute-done.2.refs_4_ = bf16[2,256,512]{2,1,0:T(8,128)(2,1)S(1)} collective-permute-done((bf16[2,256,512]{2,1,0:T(8,128)(2,1)S(1)}, bf16[2,256,512]{2,1,0:T(8,128)(2,1)S(1)}, u32[]{:S(2)}, u32[]{:S(2)}) %collective-permute-start.2) | collective-permute-done | bytes 524320 | tf_op jit(solution)/shard_map/ppermute | solution.py:144
  33.9 1.1 broadcast_select_fusion.2
  35.0 2.7 %collective-permute-start.3 = (bf16[2,256,512]{2,1,0:T(8,128)(2,1)}, bf16[2,256,512]{2,1,0:T(8,128)(2,1)S(1)}, u32[]{:S(2)}, u32[]{:S(2)}) collective-permute-start(bf16[2,256,512]{2,1,0:T(8,128)(2,1)} %get-tuple-element.86), channel_id=1, source_target_pairs={{0,1},{1,0},{2,3},{3,2},{4,5},{5,4},{6,7},{7,6},{8,9},{9,8},{10,11... | collective-permute-start | bytes 1572872 | tf_op jit(solution)/shard_map/ppermute | solution.py:150
  37.7 0.1 copy.17
  37.8 0.1 reduce-window.8
  37.9 0.1 reduce
  38.0 0.3 collective-permute-start.1
  38.3 0.1 select_reduce_fusion
  38.4 3.5 %collective-permute-done.4.refs_2_ = bf16[2,256,512]{2,1,0:T(8,128)(2,1)S(1)} collective-permute-done((bf16[2,256,512]{2,1,0:T(8,128)(2,1)S(1)}, bf16[2,256,512]{2,1,0:T(8,128)(2,1)S(1)}, u32[]{:S(2)}, u32[]{:S(2)}) %collective-permute-start.4) | collective-permute-done | bytes 524320 | tf_op jit(solution)/shard_map/ppermute | solution.py:144
  41.9 6.8 %collective-permute-done.3.refs_3_ = bf16[2,256,512]{2,1,0:T(8,128)(2,1)S(1)} collective-permute-done((bf16[2,256,512]{2,1,0:T(8,128)(2,1)}, bf16[2,256,512]{2,1,0:T(8,128)(2,1)S(1)}, u32[]{:S(2)}, u32[]{:S(2)}) %collective-permute-start.3) | collective-permute-done | bytes 524320 | tf_op jit(solution)/shard_map/ppermute | solution.py:150
  48.8 1.9 collective-permute-start.5
  50.7 1.0 broadcast_select_fusion.1
  51.7 2.8 %collective-permute-start.6 = (bf16[2,256,512]{2,1,0:T(8,128)(2,1)S(1)}, bf16[2,256,512]{2,1,0:T(8,128)(2,1)S(1)}, u32[]{:S(2)}, u32[]{:S(2)}) collective-permute-start(bf16[2,256,512]{2,1,0:T(8,128)(2,1)S(1)} %broadcast_select_fusion.1), channel_id=1, source_target_pairs={{0,1},{1,0},{2,3},{3,2},{4,5},{5,4},{6,7},{7,6},{8,9},{9,8},{10,11... | collective-permute-start | bytes 1572872 | tf_op jit(solution)/shard_map/ppermute | solution.py:150
  54.5 5.5 %collective-permute-done.1.refs_1_ = bf16[2,256,512]{2,1,0:T(8,128)(2,1)S(1)} collective-permute-done((bf16[2,256,512]{2,1,0:T(8,128)(2,1)}, bf16[2,256,512]{2,1,0:T(8,128)(2,1)S(1)}, u32[]{:S(2)}, u32[]{:S(2)}) %collective-permute-start.1) | collective-permute-done | bytes 524320 | tf_op jit(solution)/shard_map/ppermute | solution.py:150
  60.0 16.5 %shard_map.84 = (bf16[256,6144]{1,0:T(8,128)(2,1)}, bf16[256,6144]{1,0:T(8,128)(2,1)}, bf16[2,256,256]{2,1,0:T(8,128)(2,1)S(1)}, bf16[2,256,256]{2,1,0:T(8,128)(...) custom-call(s32[1,256]{1,0:T(1,128)S(1)} %bitcast.14, ...), custom_call_target="tpu_custom_call" | custom-call | flops 12079595520 | bytes 5767168 | tf_op jit(solution)/shard_map/pallas_call | solution.py:115
  76.5 0.1 broadcast_select_fusion
  76.6 3.0 %collective-permute-start.7 = (bf16[2,256,512]{2,1,0:T(8,128)(2,1)S(1)}, bf16[2,256,512]{2,1,0:T(8,128)(2,1)S(1)}, u32[]{:S(2)}, u32[]{:S(2)}) collective-permute-start(bf16[2,256,512]{2,1,0:T(8,128)(2,1)S(1)} %broadcast_select_fusion), channel_id=1, source_target_pairs={{0,1},{1,0},{2,3},{3,2},{4,5},{5,4},{6,7},{7,6},{8,9},{9,8},{10,11... | collective-permute-start | bytes 1572872 | tf_op jit(solution)/shard_map/ppermute | solution.py:150
  79.6 16.5 %shard_map.85 = (bf16[256,6144]{1,0:T(8,128)(2,1)}, bf16[256,6144]{1,0:T(8,128)(2,1)}, bf16[2,256,256]{2,1,0:T(8,128)(2,1)S(1)}, bf16[2,256,256]{2,1,0:T(8,128)(...) custom-call(s32[1,256]{1,0:T(1,128)S(1)} %bitcast.15, ...), custom_call_target="tpu_custom_call", output_to_operand_aliasing={{0}: (8, {}), {1}: (9, {})} | custom-call | flops 12079595520 | bytes 5767168 | tf_op jit(solution)/shard_map/pallas_call | solution.py:115
  96.2 0.5 collective-permute-start.8
  96.7 0.0 collective-permute-done.7.refs_3_
  96.7 16.5 %shard_map.86 = (bf16[256,6144]{1,0:T(8,128)(2,1)}, bf16[256,6144]{1,0:T(8,128)(2,1)}, bf16[2,256,256]{2,1,0:T(8,128)(2,1)S(1)}, bf16[2,256,256]{2,1,0:T(8,128)(...) custom-call(s32[1,256]{1,0:T(1,128)S(1)} %bitcast.16, ...), custom_call_target="tpu_custom_call", output_to_operand_aliasing={{0}: (8, {}), {1}: (9, {})} | custom-call | flops 12079595520 | bytes 5767168 | tf_op jit(solution)/shard_map/pallas_call | solution.py:115
  113.3 0.0 collective-permute-done.8
  113.3 16.8 %shard_map.87 = (bf16[256,6144]{1,0:T(8,128)(2,1)}, bf16[256,6144]{1,0:T(8,128)(2,1)}, bf16[2,256,256]{2,1,0:T(8,128)(2,1)S(1)}, bf16[2,256,256]{2,1,0:T(8,128)(...) custom-call(s32[1,256]{1,0:T(1,128)S(1)} %bitcast.17, ...), custom_call_target="tpu_custom_call", output_to_operand_aliasing={{0}: (8, {}), {1}: (9, {})} | custom-call | flops 12079595520 | bytes 5767168 | tf_op jit(solution)/shard_map/pallas_call | solution.py:115
  130.1 2.8 %collective-permute-start.12 = (bf16[2,256,512]{2,1,0:T(8,128)(2,1)S(1)}, bf16[2,256,512]{2,1,0:T(8,128)(2,1)S(1)}, u32[]{:S(2)}, u32[]{:S(2)}) collective-permute-start(bf16[2,256,512]{2,1,0:T(8,128)(2,1)S(1)} %pad_maximum_fusion.6), channel_id=1, source_target_pairs={{0,1},{1,0},{2,3},{3,2},{4,5},{5,4},{6,7},{7,6},{8,9},{9,8},{10,11... | collective-permute-start | bytes 1572872 | tf_op jit(solution)/shard_map/ppermute | solution.py:150
  133.0 0.2 fusion.7
  133.2 13.5 %collective-permute-start.10 = (bf16[2,256,512]{2,1,0:T(8,128)(2,1)S(1)}, bf16[2,256,512]{2,1,0:T(8,128)(2,1)S(1)}, u32[]{:S(2)}, u32[]{:S(2)}) collective-permute-start(bf16[2,256,512]{2,1,0:T(8,128)(2,1)S(1)} %fusion.7), channel_id=1, source_target_pairs={{2,0},{3,1},{4,2},{5,3},{6,4},{7,5},{8,6},{9,7},{10,8},{11,9},{12,... | collective-permute-start | bytes 1572872 | tf_op jit(solution)/shard_map/ppermute | solution.py:144
  146.7 0.3 collective-permute-start.9
  147.0 0.2 fusion.15
  147.2 12.8 %collective-permute-start.14 = (bf16[2,256,512]{2,1,0:T(8,128)(2,1)S(1)}, bf16[2,256,512]{2,1,0:T(8,128)(2,1)S(1)}, u32[]{:S(2)}, u32[]{:S(2)}) collective-permute-start(bf16[2,256,512]{2,1,0:T(8,128)(2,1)S(1)} %fusion.15), channel_id=1, source_target_pairs={{2,0},{3,1},{4,2},{5,3},{6,4},{7,5},{8,6},{9,7},{10,8},{11,9},{12,... | collective-permute-start | bytes 1572872 | tf_op jit(solution)/shard_map/ppermute | solution.py:144
  160.0 2.8 %collective-permute-start.13 = (bf16[2,256,512]{2,1,0:T(8,128)(2,1)S(1)}, bf16[2,256,512]{2,1,0:T(8,128)(2,1)S(1)}, u32[]{:S(2)}, u32[]{:S(2)}) collective-permute-start(bf16[2,256,512]{2,1,0:T(8,128)(2,1)S(1)} %pad_maximum_fusion.5), channel_id=1, source_target_pairs={{0,1},{1,0},{2,3},{3,2},{4,5},{5,4},{6,7},{7,6},{8,9},{9,8},{10,11... | collective-permute-start | bytes 1572872 | tf_op jit(solution)/shard_map/ppermute | solution.py:150
  162.8 0.0 collective-permute-done.10
  162.8 0.3 fusion.5
  163.1 7.3 %collective-permute-start.11 = (bf16[2,256,512]{2,1,0:T(8,128)(2,1)S(1)}, bf16[2,256,512]{2,1,0:T(8,128)(2,1)S(1)}, u32[]{:S(2)}, u32[]{:S(2)}) collective-permute-start(bf16[2,256,512]{2,1,0:T(8,128)(2,1)S(1)} %fusion.5), channel_id=1, source_target_pairs={{2,0},{3,1},{4,2},{5,3},{6,4},{7,5},{8,6},{9,7},{10,8},{11,9},{12,... | collective-permute-start | bytes 1572872 | tf_op jit(solution)/shard_map/ppermute | solution.py:144
  170.4 0.8 collective-permute-done.14
  171.2 0.3 fusion.13
  171.5 7.7 %collective-permute-start.15 = (bf16[2,256,512]{2,1,0:T(8,128)(2,1)S(1)}, bf16[2,256,512]{2,1,0:T(8,128)(2,1)S(1)}, u32[]{:S(2)}, u32[]{:S(2)}) collective-permute-start(bf16[2,256,512]{2,1,0:T(8,128)(2,1)S(1)} %fusion.13), channel_id=1, source_target_pairs={{2,0},{3,1},{4,2},{5,3},{6,4},{7,5},{8,6},{9,7},{10,8},{11,9},{12,... | collective-permute-start | bytes 1572872 | tf_op jit(solution)/shard_map/ppermute | solution.py:144
  179.2 0.2 fusion.2
  179.4 14.3 %collective-permute-done.15 = bf16[2,256,512]{2,1,0:T(8,128)(2,1)S(1)} collective-permute-done((bf16[2,256,512]{2,1,0:T(8,128)(2,1)S(1)}, bf16[2,256,512]{2,1,0:T(8,128)(2,1)S(1)}, u32[]{:S(2)}, u32[]{:S(2)}) %collective-permute-start.15) | collective-permute-done | bytes 524320 | tf_op jit(solution)/shard_map/ppermute | solution.py:144
  193.7 0.2 fusion.10
  193.9 1.1 fusion.18
  (15 shorter events, 0.2 us)
Async XLA Ops:
  0.6 37.1 %copy-start.1 = (s32[64]{0:T(128)S(1)}, s32[64]{0:T(128)}, u32[]{:S(2)}) copy-start(s32[64]{0:T(128)} %param.9) | copy-start | bytes 772
  1.9 19.1 %copy-start = (bf16[1,256,512]{2,1,0:T(8,128)(2,1)}, bf16[1,256,512]{2,1,0:T(8,128)(2,1)S(1)}, u32[]{:S(2)}) copy-start(bf16[1,256,512]{2,1,0:T(8,128)(2,1)S(1)} %get-tuple-element.92) | copy-start | bytes 786436
  2.0 16.4 %collective-permute-start = (bf16[2,256,512]{2,1,0:T(8,128)(2,1)S(1)}, bf16[2,256,512]{2,1,0:T(8,128)(2,1)S(1)}, u32[]{:S(2)}, u32[]{:S(2)}) collective-permute-start(bf16[2,256,512]{2,1,0:T(8,128)(2,1)S(1)} %pad_maximum_fusion.2.refs_0_), channel_id=1, source_target_pairs={{0,2},{1,3},{2,4},{3,5},{4,6},{5,7},{6,8},{7,9},{8,10},{9,11},{10,... | collective-permute-start | bytes 1572872 | tf_op jit(solution)/shard_map/ppermute | solution.py:144
  18.3 15.5 %collective-permute-start.2 = (bf16[2,256,512]{2,1,0:T(8,128)(2,1)S(1)}, bf16[2,256,512]{2,1,0:T(8,128)(2,1)S(1)}, u32[]{:S(2)}, u32[]{:S(2)}) collective-permute-start(bf16[2,256,512]{2,1,0:T(8,128)(2,1)S(1)} %collective-permute-done.refs_2_), channel_id=1, source_target_pairs={{0,2},{1,3},{2,4},{3,5},{4,6},{5,7},{6,8},{7,9},{8,10},{9,11},{10,... | collective-permute-start | bytes 1572872 | tf_op jit(solution)/shard_map/ppermute | solution.py:144
  21.1 20.8 %collective-permute-start.4 = (bf16[2,256,512]{2,1,0:T(8,128)(2,1)S(1)}, bf16[2,256,512]{2,1,0:T(8,128)(2,1)S(1)}, u32[]{:S(2)}, u32[]{:S(2)}) collective-permute-start(bf16[2,256,512]{2,1,0:T(8,128)(2,1)S(1)} %pad_maximum_fusion.1.refs_0_), channel_id=1, source_target_pairs={{0,2},{1,3},{2,4},{3,5},{4,6},{5,7},{6,8},{7,9},{8,10},{9,11},{10,... | collective-permute-start | bytes 1572872 | tf_op jit(solution)/shard_map/ppermute | solution.py:144
  35.0 13.8 %collective-permute-start.3 = (bf16[2,256,512]{2,1,0:T(8,128)(2,1)}, bf16[2,256,512]{2,1,0:T(8,128)(2,1)S(1)}, u32[]{:S(2)}, u32[]{:S(2)}) collective-permute-start(bf16[2,256,512]{2,1,0:T(8,128)(2,1)} %get-tuple-element.86), channel_id=1, source_target_pairs={{0,1},{1,0},{2,3},{3,2},{4,5},{5,4},{6,7},{7,6},{8,9},{9,8},{10,11... | collective-permute-start | bytes 1572872 | tf_op jit(solution)/shard_map/ppermute | solution.py:150
  38.0 22.0 %collective-permute-start.1 = (bf16[2,256,512]{2,1,0:T(8,128)(2,1)}, bf16[2,256,512]{2,1,0:T(8,128)(2,1)S(1)}, u32[]{:S(2)}, u32[]{:S(2)}) collective-permute-start(bf16[2,256,512]{2,1,0:T(8,128)(2,1)} %get-tuple-element.87), channel_id=1, source_target_pairs={{0,1},{1,0},{2,3},{3,2},{4,5},{5,4},{6,7},{7,6},{8,9},{9,8},{10,11... | collective-permute-start | bytes 1572872 | tf_op jit(solution)/shard_map/ppermute | solution.py:150
  48.8 27.8 %collective-permute-start.5 = (bf16[2,256,512]{2,1,0:T(8,128)(2,1)S(1)}, bf16[2,256,512]{2,1,0:T(8,128)(2,1)S(1)}, u32[]{:S(2)}, u32[]{:S(2)}) collective-permute-start(bf16[2,256,512]{2,1,0:T(8,128)(2,1)S(1)} %collective-permute-done.4.refs_2_), channel_id=1, source_target_pairs={{0,2},{1,3},{2,4},{3,5},{4,6},{5,7},{6,8},{7,9},{8,10},{9,11},{10,... | collective-permute-start | bytes 1572872 | tf_op jit(solution)/shard_map/ppermute | solution.py:144
  51.7 24.8 %collective-permute-start.6 = (bf16[2,256,512]{2,1,0:T(8,128)(2,1)S(1)}, bf16[2,256,512]{2,1,0:T(8,128)(2,1)S(1)}, u32[]{:S(2)}, u32[]{:S(2)}) collective-permute-start(bf16[2,256,512]{2,1,0:T(8,128)(2,1)S(1)} %broadcast_select_fusion.1), channel_id=1, source_target_pairs={{0,1},{1,0},{2,3},{3,2},{4,5},{5,4},{6,7},{7,6},{8,9},{9,8},{10,11... | collective-permute-start | bytes 1572872 | tf_op jit(solution)/shard_map/ppermute | solution.py:150
  76.6 20.1 %collective-permute-start.7 = (bf16[2,256,512]{2,1,0:T(8,128)(2,1)S(1)}, bf16[2,256,512]{2,1,0:T(8,128)(2,1)S(1)}, u32[]{:S(2)}, u32[]{:S(2)}) collective-permute-start(bf16[2,256,512]{2,1,0:T(8,128)(2,1)S(1)} %broadcast_select_fusion), channel_id=1, source_target_pairs={{0,1},{1,0},{2,3},{3,2},{4,5},{5,4},{6,7},{7,6},{8,9},{9,8},{10,11... | collective-permute-start | bytes 1572872 | tf_op jit(solution)/shard_map/ppermute | solution.py:150
  96.2 17.1 %collective-permute-start.8 = (bf16[2,256,512]{2,1,0:T(8,128)(2,1)S(1)}, bf16[2,256,512]{2,1,0:T(8,128)(2,1)S(1)}, u32[]{:S(2)}, u32[]{:S(2)}) collective-permute-start(bf16[2,256,512]{2,1,0:T(8,128)(2,1)S(1)} %pad_maximum_fusion.3), channel_id=1, source_target_pairs={{0,1},{1,0},{2,3},{3,2},{4,5},{5,4},{6,7},{7,6},{8,9},{9,8},{10,11... | collective-permute-start | bytes 1572872 | tf_op jit(solution)/shard_map/ppermute | solution.py:150
  130.1 16.9 %collective-permute-start.12 = (bf16[2,256,512]{2,1,0:T(8,128)(2,1)S(1)}, bf16[2,256,512]{2,1,0:T(8,128)(2,1)S(1)}, u32[]{:S(2)}, u32[]{:S(2)}) collective-permute-start(bf16[2,256,512]{2,1,0:T(8,128)(2,1)S(1)} %pad_maximum_fusion.6), channel_id=1, source_target_pairs={{0,1},{1,0},{2,3},{3,2},{4,5},{5,4},{6,7},{7,6},{8,9},{9,8},{10,11... | collective-permute-start | bytes 1572872 | tf_op jit(solution)/shard_map/ppermute | solution.py:150
  133.2 29.6 %collective-permute-start.10 = (bf16[2,256,512]{2,1,0:T(8,128)(2,1)S(1)}, bf16[2,256,512]{2,1,0:T(8,128)(2,1)S(1)}, u32[]{:S(2)}, u32[]{:S(2)}) collective-permute-start(bf16[2,256,512]{2,1,0:T(8,128)(2,1)S(1)} %fusion.7), channel_id=1, source_target_pairs={{2,0},{3,1},{4,2},{5,3},{6,4},{7,5},{8,6},{9,7},{10,8},{11,9},{12,... | collective-permute-start | bytes 1572872 | tf_op jit(solution)/shard_map/ppermute | solution.py:144
  146.7 16.1 %collective-permute-start.9 = (bf16[2,256,512]{2,1,0:T(8,128)(2,1)S(1)}, bf16[2,256,512]{2,1,0:T(8,128)(2,1)S(1)}, u32[]{:S(2)}, u32[]{:S(2)}) collective-permute-start(bf16[2,256,512]{2,1,0:T(8,128)(2,1)S(1)} %pad_maximum_fusion.4), channel_id=1, source_target_pairs={{0,1},{1,0},{2,3},{3,2},{4,5},{5,4},{6,7},{7,6},{8,9},{9,8},{10,11... | collective-permute-start | bytes 1572872 | tf_op jit(solution)/shard_map/ppermute | solution.py:150
  147.2 24.0 %collective-permute-start.14 = (bf16[2,256,512]{2,1,0:T(8,128)(2,1)S(1)}, bf16[2,256,512]{2,1,0:T(8,128)(2,1)S(1)}, u32[]{:S(2)}, u32[]{:S(2)}) collective-permute-start(bf16[2,256,512]{2,1,0:T(8,128)(2,1)S(1)} %fusion.15), channel_id=1, source_target_pairs={{2,0},{3,1},{4,2},{5,3},{6,4},{7,5},{8,6},{9,7},{10,8},{11,9},{12,... | collective-permute-start | bytes 1572872 | tf_op jit(solution)/shard_map/ppermute | solution.py:144
  160.0 11.2 %collective-permute-start.13 = (bf16[2,256,512]{2,1,0:T(8,128)(2,1)S(1)}, bf16[2,256,512]{2,1,0:T(8,128)(2,1)S(1)}, u32[]{:S(2)}, u32[]{:S(2)}) collective-permute-start(bf16[2,256,512]{2,1,0:T(8,128)(2,1)S(1)} %pad_maximum_fusion.5), channel_id=1, source_target_pairs={{0,1},{1,0},{2,3},{3,2},{4,5},{5,4},{6,7},{7,6},{8,9},{9,8},{10,11... | collective-permute-start | bytes 1572872 | tf_op jit(solution)/shard_map/ppermute | solution.py:150
  163.1 16.1 %collective-permute-start.11 = (bf16[2,256,512]{2,1,0:T(8,128)(2,1)S(1)}, bf16[2,256,512]{2,1,0:T(8,128)(2,1)S(1)}, u32[]{:S(2)}, u32[]{:S(2)}) collective-permute-start(bf16[2,256,512]{2,1,0:T(8,128)(2,1)S(1)} %fusion.5), channel_id=1, source_target_pairs={{2,0},{3,1},{4,2},{5,3},{6,4},{7,5},{8,6},{9,7},{10,8},{11,9},{12,... | collective-permute-start | bytes 1572872 | tf_op jit(solution)/shard_map/ppermute | solution.py:144
  171.5 22.2 %collective-permute-start.15 = (bf16[2,256,512]{2,1,0:T(8,128)(2,1)S(1)}, bf16[2,256,512]{2,1,0:T(8,128)(2,1)S(1)}, u32[]{:S(2)}, u32[]{:S(2)}) collective-permute-start(bf16[2,256,512]{2,1,0:T(8,128)(2,1)S(1)} %fusion.13), channel_id=1, source_target_pairs={{2,0},{3,1},{4,2},{5,3},{6,4},{7,5},{8,6},{9,7},{10,8},{11,9},{12,... | collective-permute-start | bytes 1572872 | tf_op jit(solution)/shard_map/ppermute | solution.py:144

commit v3 on v2

--- a/solution.py
+++ b/solution.py
@@ -17,7 +17,7 @@
 SCALE = DH ** (-0.5)
 LOG2E = 1.4426950408889634
 MASKED = -1e30
-WIDE = 3
+WIDE = 6
 SPLIT = 2
 PRE = False
 TIE = True

time: 195 us -> 196 us (level)
  transfers between devices with their start and end apart: 16 -> 16, of which waited for: 7 -> 7; matrix products, arithmetic and copies ran while one was open for 2% -> 2% of each run, Pallas kernels for 25% -> 26%
where the time goes in v3:
time: 196 us
  starting transfers between devices  69.1 us (35%)
  Pallas kernels  66.9 us (34%)
  waiting for transfers between devices  52.2 us (27%)
  other arithmetic  5.11 us (3%)
    pallas_call x4, Pallas kernels, attend(): pl.pallas_call(functools.partial(attention_body, aliased), grid=(heads,),...  66.9 us
    ppermute x8, starting transfers between devices, moved(): lax.ppermute(value, AXES, [(i, i + steps) for i in range(count) if 0 <= i...  53.7 us
    ppermute x8, waiting for transfers between devices, moved(): lax.ppermute(value, AXES, [(i, i + steps) for i in range(count) if 0 <= i...  39.9 us
    ppermute x8, starting transfers between devices, swapped(): return lax.ppermute(value, AXES, [(i, i ^ 1) for i in range(count)])  15.4 us
    ppermute x8, waiting for transfers between devices, swapped(): return lax.ppermute(value, AXES, [(i, i ^ 1) for i in range(count)])  12.3 us
  transfers between devices with their start and end apart: 16, of which 7 were waited for; matrix products, arithmetic and copies ran while one was open for 2% of the time, Pallas kernels for 26%

profile of v3, /device:TPU:1, one launch (start us, length us, event | category | flops | bytes accessed | tf_op | source)
XLA Modules:
  0.0 195.5 jit_solution(15045840662067353733)
XLA Ops:
  0.6 1.3 slice_bitcast_fusion
  1.9 0.0 copy-start
  1.9 0.1 pad_maximum_fusion.2.refs_0_
  2.0 4.4 %collective-permute-start = (bf16[2,256,512]{2,1,0:T(8,128)(2,1)S(1)}, bf16[2,256,512]{2,1,0:T(8,128)(2,1)S(1)}, u32[]{:S(2)}, u32[]{:S(2)}) collective-permute-start(bf16[2,256,512]{2,1,0:T(8,128)(2,1)S(1)} %pad_maximum_fusion.2.refs_0_), channel_id=1, source_target_pairs={{0,2},{1,3},{2,4},{3,5},{4,6},{5,7},{6,8},{7,9},{8,10},{9,11},{10,... | collective-permute-start | bytes 1572872 | tf_op jit(solution)/shard_map/ppermute | solution.py:144
  6.4 12.0 %collective-permute-done.refs_2_ = bf16[2,256,512]{2,1,0:T(8,128)(2,1)S(1)} collective-permute-done((bf16[2,256,512]{2,1,0:T(8,128)(2,1)S(1)}, bf16[2,256,512]{2,1,0:T(8,128)(2,1)S(1)}, u32[]{:S(2)}, u32[]{:S(2)}) %collective-permute-start) | collective-permute-done | bytes 524320 | tf_op jit(solution)/shard_map/ppermute | solution.py:144
  18.3 2.7 %collective-permute-start.2 = (bf16[2,256,512]{2,1,0:T(8,128)(2,1)S(1)}, bf16[2,256,512]{2,1,0:T(8,128)(2,1)S(1)}, u32[]{:S(2)}, u32[]{:S(2)}) collective-permute-start(bf16[2,256,512]{2,1,0:T(8,128)(2,1)S(1)} %collective-permute-done.refs_2_), channel_id=1, source_target_pairs={{0,2},{1,3},{2,4},{3,5},{4,6},{5,7},{6,8},{7,9},{8,10},{9,11},{10,... | collective-permute-start | bytes 1572872 | tf_op jit(solution)/shard_map/ppermute | solution.py:144
  21.1 0.1 pad_maximum_fusion.1.refs_0_
  21.1 3.5 %collective-permute-start.4 = (bf16[2,256,512]{2,1,0:T(8,128)(2,1)S(1)}, bf16[2,256,512]{2,1,0:T(8,128)(2,1)S(1)}, u32[]{:S(2)}, u32[]{:S(2)}) collective-permute-start(bf16[2,256,512]{2,1,0:T(8,128)(2,1)S(1)} %pad_maximum_fusion.1.refs_0_), channel_id=1, source_target_pairs={{0,2},{1,3},{2,4},{3,5},{4,6},{5,7},{6,8},{7,9},{8,10},{9,11},{10,... | collective-permute-start | bytes 1572872 | tf_op jit(solution)/shard_map/ppermute | solution.py:144
  24.7 9.2 %collective-permute-done.2.refs_4_ = bf16[2,256,512]{2,1,0:T(8,128)(2,1)S(1)} collective-permute-done((bf16[2,256,512]{2,1,0:T(8,128)(2,1)S(1)}, bf16[2,256,512]{2,1,0:T(8,128)(2,1)S(1)}, u32[]{:S(2)}, u32[]{:S(2)}) %collective-permute-start.2) | collective-permute-done | bytes 524320 | tf_op jit(solution)/shard_map/ppermute | solution.py:144
  33.9 1.1 broadcast_select_fusion.2
  35.0 2.7 %collective-permute-start.3 = (bf16[2,256,512]{2,1,0:T(8,128)(2,1)}, bf16[2,256,512]{2,1,0:T(8,128)(2,1)S(1)}, u32[]{:S(2)}, u32[]{:S(2)}) collective-permute-start(bf16[2,256,512]{2,1,0:T(8,128)(2,1)} %get-tuple-element.86), channel_id=1, source_target_pairs={{0,1},{1,0},{2,3},{3,2},{4,5},{5,4},{6,7},{7,6},{8,9},{9,8},{10,11... | collective-permute-start | bytes 1572872 | tf_op jit(solution)/shard_map/ppermute | solution.py:150
  37.7 0.1 copy.17
  37.8 0.1 reduce-window.8
  37.9 0.1 reduce
  38.0 0.3 collective-permute-start.1
  38.3 0.1 select_reduce_fusion
  38.4 3.5 %collective-permute-done.4.refs_2_ = bf16[2,256,512]{2,1,0:T(8,128)(2,1)S(1)} collective-permute-done((bf16[2,256,512]{2,1,0:T(8,128)(2,1)S(1)}, bf16[2,256,512]{2,1,0:T(8,128)(2,1)S(1)}, u32[]{:S(2)}, u32[]{:S(2)}) %collective-permute-start.4) | collective-permute-done | bytes 524320 | tf_op jit(solution)/shard_map/ppermute | solution.py:144
  41.9 6.8 %collective-permute-done.3.refs_3_ = bf16[2,256,512]{2,1,0:T(8,128)(2,1)S(1)} collective-permute-done((bf16[2,256,512]{2,1,0:T(8,128)(2,1)}, bf16[2,256,512]{2,1,0:T(8,128)(2,1)S(1)}, u32[]{:S(2)}, u32[]{:S(2)}) %collective-permute-start.3) | collective-permute-done | bytes 524320 | tf_op jit(solution)/shard_map/ppermute | solution.py:150
  48.8 1.9 collective-permute-start.5
  50.7 1.0 broadcast_select_fusion.1
  51.7 2.8 %collective-permute-start.6 = (bf16[2,256,512]{2,1,0:T(8,128)(2,1)S(1)}, bf16[2,256,512]{2,1,0:T(8,128)(2,1)S(1)}, u32[]{:S(2)}, u32[]{:S(2)}) collective-permute-start(bf16[2,256,512]{2,1,0:T(8,128)(2,1)S(1)} %broadcast_select_fusion.1), channel_id=1, source_target_pairs={{0,1},{1,0},{2,3},{3,2},{4,5},{5,4},{6,7},{7,6},{8,9},{9,8},{10,11... | collective-permute-start | bytes 1572872 | tf_op jit(solution)/shard_map/ppermute | solution.py:150
  54.5 5.5 %collective-permute-done.1.refs_1_ = bf16[2,256,512]{2,1,0:T(8,128)(2,1)S(1)} collective-permute-done((bf16[2,256,512]{2,1,0:T(8,128)(2,1)}, bf16[2,256,512]{2,1,0:T(8,128)(2,1)S(1)}, u32[]{:S(2)}, u32[]{:S(2)}) %collective-permute-start.1) | collective-permute-done | bytes 524320 | tf_op jit(solution)/shard_map/ppermute | solution.py:150
  60.0 16.7 %shard_map.84 = (bf16[256,6144]{1,0:T(8,128)(2,1)}, bf16[256,6144]{1,0:T(8,128)(2,1)}, bf16[2,256,256]{2,1,0:T(8,128)(2,1)S(1)}, bf16[2,256,256]{2,1,0:T(8,128)(...) custom-call(s32[1,256]{1,0:T(1,128)S(1)} %bitcast.14, ...), custom_call_target="tpu_custom_call" | custom-call | flops 12079595520 | bytes 5767168 | tf_op jit(solution)/shard_map/pallas_call | solution.py:115
  76.6 0.0 collective-permute-done.6.refs_1_
  76.6 0.0 collective-permute-done.5.refs_4_
  76.7 0.1 broadcast_select_fusion
  76.7 3.0 %collective-permute-start.7 = (bf16[2,256,512]{2,1,0:T(8,128)(2,1)S(1)}, bf16[2,256,512]{2,1,0:T(8,128)(2,1)S(1)}, u32[]{:S(2)}, u32[]{:S(2)}) collective-permute-start(bf16[2,256,512]{2,1,0:T(8,128)(2,1)S(1)} %broadcast_select_fusion), channel_id=1, source_target_pairs={{0,1},{1,0},{2,3},{3,2},{4,5},{5,4},{6,7},{7,6},{8,9},{9,8},{10,11... | collective-permute-start | bytes 1572872 | tf_op jit(solution)/shard_map/ppermute | solution.py:150
  79.7 16.7 %shard_map.85 = (bf16[256,6144]{1,0:T(8,128)(2,1)}, bf16[256,6144]{1,0:T(8,128)(2,1)}, bf16[2,256,256]{2,1,0:T(8,128)(2,1)S(1)}, bf16[2,256,256]{2,1,0:T(8,128)(...) custom-call(s32[1,256]{1,0:T(1,128)S(1)} %bitcast.15, ...), custom_call_target="tpu_custom_call", output_to_operand_aliasing={{0}: (8, {}), {1}: (9, {})} | custom-call | flops 12079595520 | bytes 5767168 | tf_op jit(solution)/shard_map/pallas_call | solution.py:115
  96.4 0.5 collective-permute-start.8
  96.9 16.7 %shard_map.86 = (bf16[256,6144]{1,0:T(8,128)(2,1)}, bf16[256,6144]{1,0:T(8,128)(2,1)}, bf16[2,256,256]{2,1,0:T(8,128)(2,1)S(1)}, bf16[2,256,256]{2,1,0:T(8,128)(...) custom-call(s32[1,256]{1,0:T(1,128)S(1)} %bitcast.16, ...), custom_call_target="tpu_custom_call", output_to_operand_aliasing={{0}: (8, {}), {1}: (9, {})} | custom-call | flops 12079595520 | bytes 5767168 | tf_op jit(solution)/shard_map/pallas_call | solution.py:115
  113.6 0.0 collective-permute-done.8
  113.6 16.9 %shard_map.87 = (bf16[256,6144]{1,0:T(8,128)(2,1)}, bf16[256,6144]{1,0:T(8,128)(2,1)}, bf16[2,256,256]{2,1,0:T(8,128)(2,1)S(1)}, bf16[2,256,256]{2,1,0:T(8,128)(...) custom-call(s32[1,256]{1,0:T(1,128)S(1)} %bitcast.17, ...), custom_call_target="tpu_custom_call", output_to_operand_aliasing={{0}: (8, {}), {1}: (9, {})} | custom-call | flops 12079595520 | bytes 5767168 | tf_op jit(solution)/shard_map/pallas_call | solution.py:115
  130.6 2.8 %collective-permute-start.12 = (bf16[2,256,512]{2,1,0:T(8,128)(2,1)S(1)}, bf16[2,256,512]{2,1,0:T(8,128)(2,1)S(1)}, u32[]{:S(2)}, u32[]{:S(2)}) collective-permute-start(bf16[2,256,512]{2,1,0:T(8,128)(2,1)S(1)} %pad_maximum_fusion.6), channel_id=1, source_target_pairs={{0,1},{1,0},{2,3},{3,2},{4,5},{5,4},{6,7},{7,6},{8,9},{9,8},{10,11... | collective-permute-start | bytes 1572872 | tf_op jit(solution)/shard_map/ppermute | solution.py:150
  133.5 0.2 fusion.7
  133.6 13.5 %collective-permute-start.10 = (bf16[2,256,512]{2,1,0:T(8,128)(2,1)S(1)}, bf16[2,256,512]{2,1,0:T(8,128)(2,1)S(1)}, u32[]{:S(2)}, u32[]{:S(2)}) collective-permute-start(bf16[2,256,512]{2,1,0:T(8,128)(2,1)S(1)} %fusion.7), channel_id=1, source_target_pairs={{2,0},{3,1},{4,2},{5,3},{6,4},{7,5},{8,6},{9,7},{10,8},{11,9},{12,... | collective-permute-start | bytes 1572872 | tf_op jit(solution)/shard_map/ppermute | solution.py:144
  147.1 0.3 collective-permute-start.9
  147.5 0.2 fusion.15
  147.7 12.8 %collective-permute-start.14 = (bf16[2,256,512]{2,1,0:T(8,128)(2,1)S(1)}, bf16[2,256,512]{2,1,0:T(8,128)(2,1)S(1)}, u32[]{:S(2)}, u32[]{:S(2)}) collective-permute-start(bf16[2,256,512]{2,1,0:T(8,128)(2,1)S(1)} %fusion.15), channel_id=1, source_target_pairs={{2,0},{3,1},{4,2},{5,3},{6,4},{7,5},{8,6},{9,7},{10,8},{11,9},{12,... | collective-permute-start | bytes 1572872 | tf_op jit(solution)/shard_map/ppermute | solution.py:144
  160.4 2.8 %collective-permute-start.13 = (bf16[2,256,512]{2,1,0:T(8,128)(2,1)S(1)}, bf16[2,256,512]{2,1,0:T(8,128)(2,1)S(1)}, u32[]{:S(2)}, u32[]{:S(2)}) collective-permute-start(bf16[2,256,512]{2,1,0:T(8,128)(2,1)S(1)} %pad_maximum_fusion.5), channel_id=1, source_target_pairs={{0,1},{1,0},{2,3},{3,2},{4,5},{5,4},{6,7},{7,6},{8,9},{9,8},{10,11... | collective-permute-start | bytes 1572872 | tf_op jit(solution)/shard_map/ppermute | solution.py:150
  163.3 0.3 fusion.5
  163.5 7.2 %collective-permute-start.11 = (bf16[2,256,512]{2,1,0:T(8,128)(2,1)S(1)}, bf16[2,256,512]{2,1,0:T(8,128)(2,1)S(1)}, u32[]{:S(2)}, u32[]{:S(2)}) collective-permute-start(bf16[2,256,512]{2,1,0:T(8,128)(2,1)S(1)} %fusion.5), channel_id=1, source_target_pairs={{2,0},{3,1},{4,2},{5,3},{6,4},{7,5},{8,6},{9,7},{10,8},{11,9},{12,... | collective-permute-start | bytes 1572872 | tf_op jit(solution)/shard_map/ppermute | solution.py:144
  170.8 0.9 collective-permute-done.14
  171.7 0.3 fusion.13
  171.9 7.7 %collective-permute-start.15 = (bf16[2,256,512]{2,1,0:T(8,128)(2,1)S(1)}, bf16[2,256,512]{2,1,0:T(8,128)(2,1)S(1)}, u32[]{:S(2)}, u32[]{:S(2)}) collective-permute-start(bf16[2,256,512]{2,1,0:T(8,128)(2,1)S(1)} %fusion.13), channel_id=1, source_target_pairs={{2,0},{3,1},{4,2},{5,3},{6,4},{7,5},{8,6},{9,7},{10,8},{11,9},{12,... | collective-permute-start | bytes 1572872 | tf_op jit(solution)/shard_map/ppermute | solution.py:144
  179.7 0.2 fusion.2
  179.9 14.3 %collective-permute-done.15 = bf16[2,256,512]{2,1,0:T(8,128)(2,1)S(1)} collective-permute-done((bf16[2,256,512]{2,1,0:T(8,128)(2,1)S(1)}, bf16[2,256,512]{2,1,0:T(8,128)(2,1)S(1)}, u32[]{:S(2)}, u32[]{:S(2)}) %collective-permute-start.15) | collective-permute-done | bytes 524320 | tf_op jit(solution)/shard_map/ppermute | solution.py:144
  194.2 0.2 fusion.10
  194.4 1.1 fusion.18
  (15 shorter events, 0.2 us)
Async XLA Ops:
  0.6 37.1 %copy-start.1 = (s32[64]{0:T(128)S(1)}, s32[64]{0:T(128)}, u32[]{:S(2)}) copy-start(s32[64]{0:T(128)} %param.9) | copy-start | bytes 772
  1.9 19.1 %copy-start = (bf16[1,256,512]{2,1,0:T(8,128)(2,1)}, bf16[1,256,512]{2,1,0:T(8,128)(2,1)S(1)}, u32[]{:S(2)}) copy-start(bf16[1,256,512]{2,1,0:T(8,128)(2,1)S(1)} %get-tuple-element.92) | copy-start | bytes 786436
  2.0 16.4 %collective-permute-start = (bf16[2,256,512]{2,1,0:T(8,128)(2,1)S(1)}, bf16[2,256,512]{2,1,0:T(8,128)(2,1)S(1)}, u32[]{:S(2)}, u32[]{:S(2)}) collective-permute-start(bf16[2,256,512]{2,1,0:T(8,128)(2,1)S(1)} %pad_maximum_fusion.2.refs_0_), channel_id=1, source_target_pairs={{0,2},{1,3},{2,4},{3,5},{4,6},{5,7},{6,8},{7,9},{8,10},{9,11},{10,... | collective-permute-start | bytes 1572872 | tf_op jit(solution)/shard_map/ppermute | solution.py:144
  18.3 15.5 %collective-permute-start.2 = (bf16[2,256,512]{2,1,0:T(8,128)(2,1)S(1)}, bf16[2,256,512]{2,1,0:T(8,128)(2,1)S(1)}, u32[]{:S(2)}, u32[]{:S(2)}) collective-permute-start(bf16[2,256,512]{2,1,0:T(8,128)(2,1)S(1)} %collective-permute-done.refs_2_), channel_id=1, source_target_pairs={{0,2},{1,3},{2,4},{3,5},{4,6},{5,7},{6,8},{7,9},{8,10},{9,11},{10,... | collective-permute-start | bytes 1572872 | tf_op jit(solution)/shard_map/ppermute | solution.py:144
  21.1 20.8 %collective-permute-start.4 = (bf16[2,256,512]{2,1,0:T(8,128)(2,1)S(1)}, bf16[2,256,512]{2,1,0:T(8,128)(2,1)S(1)}, u32[]{:S(2)}, u32[]{:S(2)}) collective-permute-start(bf16[2,256,512]{2,1,0:T(8,128)(2,1)S(1)} %pad_maximum_fusion.1.refs_0_), channel_id=1, source_target_pairs={{0,2},{1,3},{2,4},{3,5},{4,6},{5,7},{6,8},{7,9},{8,10},{9,11},{10,... | collective-permute-start | bytes 1572872 | tf_op jit(solution)/shard_map/ppermute | solution.py:144
  35.0 13.8 %collective-permute-start.3 = (bf16[2,256,512]{2,1,0:T(8,128)(2,1)}, bf16[2,256,512]{2,1,0:T(8,128)(2,1)S(1)}, u32[]{:S(2)}, u32[]{:S(2)}) collective-permute-start(bf16[2,256,512]{2,1,0:T(8,128)(2,1)} %get-tuple-element.86), channel_id=1, source_target_pairs={{0,1},{1,0},{2,3},{3,2},{4,5},{5,4},{6,7},{7,6},{8,9},{9,8},{10,11... | collective-permute-start | bytes 1572872 | tf_op jit(solution)/shard_map/ppermute | solution.py:150
  38.0 22.0 %collective-permute-start.1 = (bf16[2,256,512]{2,1,0:T(8,128)(2,1)}, bf16[2,256,512]{2,1,0:T(8,128)(2,1)S(1)}, u32[]{:S(2)}, u32[]{:S(2)}) collective-permute-start(bf16[2,256,512]{2,1,0:T(8,128)(2,1)} %get-tuple-element.87), channel_id=1, source_target_pairs={{0,1},{1,0},{2,3},{3,2},{4,5},{5,4},{6,7},{7,6},{8,9},{9,8},{10,11... | collective-permute-start | bytes 1572872 | tf_op jit(solution)/shard_map/ppermute | solution.py:150
  48.8 27.9 %collective-permute-start.5 = (bf16[2,256,512]{2,1,0:T(8,128)(2,1)S(1)}, bf16[2,256,512]{2,1,0:T(8,128)(2,1)S(1)}, u32[]{:S(2)}, u32[]{:S(2)}) collective-permute-start(bf16[2,256,512]{2,1,0:T(8,128)(2,1)S(1)} %collective-permute-done.4.refs_2_), channel_id=1, source_target_pairs={{0,2},{1,3},{2,4},{3,5},{4,6},{5,7},{6,8},{7,9},{8,10},{9,11},{10,... | collective-permute-start | bytes 1572872 | tf_op jit(solution)/shard_map/ppermute | solution.py:144
  51.7 24.9 %collective-permute-start.6 = (bf16[2,256,512]{2,1,0:T(8,128)(2,1)S(1)}, bf16[2,256,512]{2,1,0:T(8,128)(2,1)S(1)}, u32[]{:S(2)}, u32[]{:S(2)}) collective-permute-start(bf16[2,256,512]{2,1,0:T(8,128)(2,1)S(1)} %broadcast_select_fusion.1), channel_id=1, source_target_pairs={{0,1},{1,0},{2,3},{3,2},{4,5},{5,4},{6,7},{7,6},{8,9},{9,8},{10,11... | collective-permute-start | bytes 1572872 | tf_op jit(solution)/shard_map/ppermute | solution.py:150
  76.7 20.2 %collective-permute-start.7 = (bf16[2,256,512]{2,1,0:T(8,128)(2,1)S(1)}, bf16[2,256,512]{2,1,0:T(8,128)(2,1)S(1)}, u32[]{:S(2)}, u32[]{:S(2)}) collective-permute-start(bf16[2,256,512]{2,1,0:T(8,128)(2,1)S(1)} %broadcast_select_fusion), channel_id=1, source_target_pairs={{0,1},{1,0},{2,3},{3,2},{4,5},{5,4},{6,7},{7,6},{8,9},{9,8},{10,11... | collective-permute-start | bytes 1572872 | tf_op jit(solution)/shard_map/ppermute | solution.py:150
  96.4 17.2 %collective-permute-start.8 = (bf16[2,256,512]{2,1,0:T(8,128)(2,1)S(1)}, bf16[2,256,512]{2,1,0:T(8,128)(2,1)S(1)}, u32[]{:S(2)}, u32[]{:S(2)}) collective-permute-start(bf16[2,256,512]{2,1,0:T(8,128)(2,1)S(1)} %pad_maximum_fusion.3), channel_id=1, source_target_pairs={{0,1},{1,0},{2,3},{3,2},{4,5},{5,4},{6,7},{7,6},{8,9},{9,8},{10,11... | collective-permute-start | bytes 1572872 | tf_op jit(solution)/shard_map/ppermute | solution.py:150
  130.6 16.9 %collective-permute-start.12 = (bf16[2,256,512]{2,1,0:T(8,128)(2,1)S(1)}, bf16[2,256,512]{2,1,0:T(8,128)(2,1)S(1)}, u32[]{:S(2)}, u32[]{:S(2)}) collective-permute-start(bf16[2,256,512]{2,1,0:T(8,128)(2,1)S(1)} %pad_maximum_fusion.6), channel_id=1, source_target_pairs={{0,1},{1,0},{2,3},{3,2},{4,5},{5,4},{6,7},{7,6},{8,9},{9,8},{10,11... | collective-permute-start | bytes 1572872 | tf_op jit(solution)/shard_map/ppermute | solution.py:150
  133.6 29.6 %collective-permute-start.10 = (bf16[2,256,512]{2,1,0:T(8,128)(2,1)S(1)}, bf16[2,256,512]{2,1,0:T(8,128)(2,1)S(1)}, u32[]{:S(2)}, u32[]{:S(2)}) collective-permute-start(bf16[2,256,512]{2,1,0:T(8,128)(2,1)S(1)} %fusion.7), channel_id=1, source_target_pairs={{2,0},{3,1},{4,2},{5,3},{6,4},{7,5},{8,6},{9,7},{10,8},{11,9},{12,... | collective-permute-start | bytes 1572872 | tf_op jit(solution)/shard_map/ppermute | solution.py:144
  147.1 16.1 %collective-permute-start.9 = (bf16[2,256,512]{2,1,0:T(8,128)(2,1)S(1)}, bf16[2,256,512]{2,1,0:T(8,128)(2,1)S(1)}, u32[]{:S(2)}, u32[]{:S(2)}) collective-permute-start(bf16[2,256,512]{2,1,0:T(8,128)(2,1)S(1)} %pad_maximum_fusion.4), channel_id=1, source_target_pairs={{0,1},{1,0},{2,3},{3,2},{4,5},{5,4},{6,7},{7,6},{8,9},{9,8},{10,11... | collective-permute-start | bytes 1572872 | tf_op jit(solution)/shard_map/ppermute | solution.py:150
  147.7 24.0 %collective-permute-start.14 = (bf16[2,256,512]{2,1,0:T(8,128)(2,1)S(1)}, bf16[2,256,512]{2,1,0:T(8,128)(2,1)S(1)}, u32[]{:S(2)}, u32[]{:S(2)}) collective-permute-start(bf16[2,256,512]{2,1,0:T(8,128)(2,1)S(1)} %fusion.15), channel_id=1, source_target_pairs={{2,0},{3,1},{4,2},{5,3},{6,4},{7,5},{8,6},{9,7},{10,8},{11,9},{12,... | collective-permute-start | bytes 1572872 | tf_op jit(solution)/shard_map/ppermute | solution.py:144
  160.4 11.2 %collective-permute-start.13 = (bf16[2,256,512]{2,1,0:T(8,128)(2,1)S(1)}, bf16[2,256,512]{2,1,0:T(8,128)(2,1)S(1)}, u32[]{:S(2)}, u32[]{:S(2)}) collective-permute-start(bf16[2,256,512]{2,1,0:T(8,128)(2,1)S(1)} %pad_maximum_fusion.5), channel_id=1, source_target_pairs={{0,1},{1,0},{2,3},{3,2},{4,5},{5,4},{6,7},{7,6},{8,9},{9,8},{10,11... | collective-permute-start | bytes 1572872 | tf_op jit(solution)/shard_map/ppermute | solution.py:150
  163.5 16.1 %collective-permute-start.11 = (bf16[2,256,512]{2,1,0:T(8,128)(2,1)S(1)}, bf16[2,256,512]{2,1,0:T(8,128)(2,1)S(1)}, u32[]{:S(2)}, u32[]{:S(2)}) collective-permute-start(bf16[2,256,512]{2,1,0:T(8,128)(2,1)S(1)} %fusion.5), channel_id=1, source_target_pairs={{2,0},{3,1},{4,2},{5,3},{6,4},{7,5},{8,6},{9,7},{10,8},{11,9},{12,... | collective-permute-start | bytes 1572872 | tf_op jit(solution)/shard_map/ppermute | solution.py:144
  171.9 22.2 %collective-permute-start.15 = (bf16[2,256,512]{2,1,0:T(8,128)(2,1)S(1)}, bf16[2,256,512]{2,1,0:T(8,128)(2,1)S(1)}, u32[]{:S(2)}, u32[]{:S(2)}) collective-permute-start(bf16[2,256,512]{2,1,0:T(8,128)(2,1)S(1)} %fusion.13), channel_id=1, source_target_pairs={{2,0},{3,1},{4,2},{5,3},{6,4},{7,5},{8,6},{9,7},{10,8},{11,9},{12,... | collective-permute-start | bytes 1572872 | tf_op jit(solution)/shard_map/ppermute | solution.py:144
